TPU v7x, 128 devices: a whole 4x4x4 slice. The times are simulated.
128 devices in a mesh: dp: 16 (over z_lo, x, core), mp: 8 (over y, z_hi).
Axes of the slice: x: 4, y: 4, z: 4 (z_hi: 2, z_lo: 2; z = z_hi * 2 + z_lo), core: 2. Of those that a mesh axis runs over, the one named last changes fastest.
Arguments:
- tokens: bfloat16 [1024, 18432], P('mp', 'dp'), may hold values from -6 to 6
- gate_weight: bfloat16 [18432, 8192], P('dp', 'mp'), may hold values from -0.046875 to 0.046875
- up_weight: bfloat16 [18432, 8192], P('dp', 'mp'), may hold values from -0.046875 to 0.046875
- down_weight: bfloat16 [8192, 18432], P('mp', 'dp'), may hold values from -0.0625 to 0.0625
- cotangent: bfloat16 [1024, 18432], P('mp', 'dp'), may hold values from -1.5 to 1.5
Outputs:
- mixed: bfloat16 [1024, 18432], P('mp', 'dp')
- grad_tokens: bfloat16 [1024, 18432], P('mp', 'dp')
- grad_gate: float32 [18432, 8192], P('dp', 'mp')
- grad_up: float32 [18432, 8192], P('dp', 'mp')
- grad_down: float32 [8192, 18432], P('mp', 'dp')
All inputs are finite; a program needn't handle non-finite values.
Results may differ from a plain program's by a relative error of at most 0.0049.
Values may be sent and summed in bfloat16 or wider, within the bound.
A program may use at most 128 MiB of HBM per device.

v0:
```python
import jax
import jax.numpy as jnp
from jax import lax
from jax.sharding import PartitionSpec as P


def times_transposed(left, right):
    return lax.dot_general(
        left, right, (((1,), (1,)), ((), ())), preferred_element_type=jnp.float32
    )


def inner_rows(left, right):
    return lax.dot_general(
        left, right, (((0,), (0,)), ((), ())), preferred_element_type=jnp.float32
    )


def on_device(tokens, gate_weight, up_weight, down_weight, cotangent):
    rows_all = lax.all_gather(tokens, "mp", axis=0, tiled=True)
    width = gate_weight.shape[1]
    block = rows_all
    joined = lax.psum(
        jnp.concatenate(
            [
                jnp.dot(block, gate_weight, preferred_element_type=jnp.float32),
                jnp.dot(block, up_weight, preferred_element_type=jnp.float32),
            ],
            axis=1,
        ),
        "dp",
    )
    gate = joined[:, :width]
    up = joined[:, width:]
    sigma = jax.nn.sigmoid(gate)
    hidden_part = (gate * sigma * up).astype(jnp.bfloat16)
    block = hidden_part
    mixed = lax.psum_scatter(
        jnp.dot(block, down_weight, preferred_element_type=jnp.float32),
        "mp",
        scatter_dimension=0,
        tiled=True,
    ).astype(jnp.bfloat16)
    cot_all = lax.all_gather(cotangent, "mp", axis=0, tiled=True)
    block = cot_all
    grad_hidden = lax.psum(times_transposed(block, down_weight), "dp")
    grad_gate_pre = (grad_hidden * up * sigma * (1.0 + gate * (1.0 - sigma))).astype(jnp.bfloat16)
    grad_up_pre = (grad_hidden * gate * sigma).astype(jnp.bfloat16)
    grad_tokens = lax.psum_scatter(
        times_transposed(grad_gate_pre, gate_weight) + times_transposed(grad_up_pre, up_weight),
        "mp",
        scatter_dimension=0,
        tiled=True,
    ).astype(jnp.bfloat16)
    grad_gate = inner_rows(rows_all, grad_gate_pre)
    grad_up = inner_rows(rows_all, grad_up_pre)
    grad_down = inner_rows(hidden_part, cot_all)
    return (mixed, grad_tokens, grad_gate, grad_up, grad_down)


def solution(mesh):
    in_specs = (P("mp", "dp"), P("dp", "mp"), P("dp", "mp"), P("mp", "dp"), P("mp", "dp"))
    out_specs = (P("mp", "dp"), P("mp", "dp"), P("dp", "mp"), P("dp", "mp"), P("mp", "dp"))
    return jax.shard_map(
        on_device, mesh=mesh, in_specs=in_specs, out_specs=out_specs, check_vma=False
    )
```

profile of v0, /device:TPU:0, one launch (start us, length us, event | category | flops | bytes accessed | tf_op | source)
XLA Modules:
  0.0 493.5 jit_solution(16951094734319080455)
XLA Ops:
  7.2 0.0 copy-start
  7.2 0.0 all-gather.3.cloned.1.call-start
  7.2 0.7 all-gather.3.cloned.1.call-update
  7.9 0.0 all-gather.5.cloned.1.call-start
  8.0 0.7 all-gather.5.cloned.1.call-update
  8.7 0.0 all-reduce.3.cloned.1.call-start
  8.7 61.0 %all-gather.3.cloned.1.call-done = bf16[1024,1152]{1,0:T(8,128)(2,1)} async-done(((bf16[128,1152]{1,0:T(8,128)(2,1)}), bf16[1024,1152]{1,0:T(8,128)(2,1)}) %all-gather.3.cloned.1.call-update) | async-done | bytes 2359312 | tf_op jit(solution)/shard_map/all_gather | solution.py:20
  69.7 0.0 copy-start.5
  69.7 0.0 copy-start.7
  69.7 5.5 %fusion.1 = f32[1024,1024]{0,1:T(8,128)S(1)} fusion(bf16[1024,1152]{1,0:T(8,128)(2,1)} %all-gather.3.cloned.1.call-done, bf16[1152,1024]{1,0:T(8,128)(2,1)} %param.7), kind=kOutput, calls=%fused_computation.9 | convolution fusion | flops 2415919104 | bytes 8912896 | tf_op jit(solution)/shard_map/dot_general | solution.py:27
  75.2 0.0 copy-done.5
  75.2 0.0 copy-done.7
  75.2 2.9 fusion
  78.1 4.1 pad_maximum_fusion
  82.2 45.4 %all-gather.5.cloned.1.call-done = bf16[1024,1152]{1,0:T(8,128)(2,1)} async-done(((bf16[128,1152]{1,0:T(8,128)(2,1)}), bf16[1024,1152]{1,0:T(8,128)(2,1)}) %all-gather.5.cloned.1.call-update) | async-done | bytes 2359312 | tf_op jit(solution)/shard_map/all_gather | solution.py:44
  127.6 0.0 copy-done
  127.6 6.1 %fusion.3 = f32[1024,1024]{0,1:T(8,128)} fusion(bf16[1024,1152]{1,0:T(8,128)(2,1)} %all-gather.5.cloned.1.call-done, bf16[1024,1152]{1,0:T(8,128)(2,1)S(1)} %copy-done), kind=kOutput, calls=%fused_computation.11 | convolution fusion | flops 2415919104 | bytes 8912896 | tf_op jit(solution)/shard_map/dot_general | solution.py:8
  133.7 0.0 all-reduce.3.cloned.1.call-update
  133.7 0.0 reduce-scatter.3.cloned.1.call-start
  133.8 158.1 %all-reduce.3.cloned.1.call-done = (f32[1024,2048]{0,1:T(8,128)}, f32[1024,1024]{0,1:T(8,128)}) async-done(((f32[1024,2048]{0,1:T(8,128)}, f32[1024,1024]{0,1:T(8,128)}), (f32[1024,2048]{0,1:T(8,128)}, f32[1024,1024]{0,1:T(8,128)})) %all-reduce.3.cloned.1.call-update) | async-done | bytes 12582928 | tf_op jit(solution)/shard_map/psum | solution.py:23
  291.9 7.3 %multiply_convert_fusion = (bf16[1024,1024]{0,1:T(8,128)(2,1)}, bf16[1024,1024]{0,1:T(8,128)(2,1)}, bf16[1024,1024]{0,1:T(8,128)(2,1)S(1)}) fusion(f32[1024,1024]{0,1:T(8,128)} %get-tuple-element.11, f32[1024,2048]{0,1:T(8,128)} %get-tuple-element.10), kind=kLoop, calls=%fused_computation.4 | loop fusion | flops 16777216 | bytes 18874368 | tf_op jit(solution)/shard_map/convert_element_type | solution.py:48
  299.2 0.0 copy-start.2
  299.2 1.3 copy-done.2
  300.6 4.6 fusion.2
  305.2 0.0 copy-start.3
  305.2 0.0 reduce-scatter.3.cloned.1.call-update
  305.2 0.2 reduce-scatter.5.cloned.1.call-start
  305.4 1.3 copy-done.3
  306.8 0.0 copy-start.4
  306.8 0.0 copy-start.6
  306.8 4.7 fusion.4
  311.5 0.0 copy-done.4
  311.5 0.0 copy-done.6
  311.5 4.7 convolution_add_fusion
  316.3 0.0 reduce-scatter.5.cloned.1.call-update
  316.3 7.4 %convolution_bitcast_fusion = f32[1152,1024]{0,1:T(8,128)} fusion(bf16[1024,1024]{0,1:T(8,128)(2,1)} %get-tuple-element.12, bf16[1024,1152]{1,0:T(8,128)(2,1)} %all-gather.3.cloned.1.call-done), kind=kOutput, calls=%fused_computation.2 | convolution fusion | flops 2415919104 | bytes 9175040 | tf_op jit(solution)/shard_map/dot_general | solution.py:14
  323.6 6.1 %copy.12 = f32[1152,1024]{1,0:T(8,128)} copy(f32[1152,1024]{0,1:T(8,128)} %convolution_bitcast_fusion) | data formatting | bytes 9437184
  329.7 6.1 %convolution_bitcast_fusion.1 = f32[1152,1024]{0,1:T(8,128)} fusion(bf16[1024,1024]{0,1:T(8,128)(2,1)S(1)} %copy-done.3, bf16[1024,1152]{1,0:T(8,128)(2,1)} %all-gather.3.cloned.1.call-done), kind=kOutput, calls=%fused_computation.3 | convolution fusion | flops 2415919104 | bytes 9175040 | tf_op jit(solution)/shard_map/dot_general | solution.py:14
  335.9 6.1 %copy.11 = f32[1152,1024]{1,0:T(8,128)} copy(f32[1152,1024]{0,1:T(8,128)} %convolution_bitcast_fusion.1) | data formatting | bytes 9437184
  341.9 0.0 copy-start.1
  341.9 7.6 %fusion.5 = f32[1024,1152]{1,0:T(8,128)} fusion(bf16[1024,1024]{0,1:T(8,128)(2,1)} %copy-done.2, bf16[1024,1152]{1,0:T(8,128)(2,1)} %all-gather.5.cloned.1.call-done), kind=kOutput, calls=%fused_computation.13 | convolution fusion | flops 2415919104 | bytes 9175040 | tf_op jit(solution)/shard_map/dot_general | solution.py:14
  349.5 44.1 %reduce-scatter.3.cloned.1.call-done = f32[128,1152]{1,0:T(8,128)} async-done(((f32[1024,1152]{1,0:T(8,128)}), f32[128,1152]{1,0:T(8,128)}) %reduce-scatter.3.cloned.1.call-update) | async-done | bytes 589840 | tf_op jit(solution)/shard_map/reduce_scatter | solution.py:38
  393.7 1.8 convert_element_type.16
  395.5 89.7 %reduce-scatter.5.cloned.1.call-done = f32[128,1152]{1,0:T(8,128)} async-done(((f32[1024,1152]{1,0:T(8,128)}), f32[128,1152]{1,0:T(8,128)}) %reduce-scatter.5.cloned.1.call-update) | async-done | bytes 589840 | tf_op jit(solution)/shard_map/reduce_scatter | solution.py:49
  485.2 1.8 convert_element_type.19
  487.0 0.0 copy-done.1
Async XLA Ops:
  7.2 120.5 %copy-start = (bf16[1024,1152]{1,0:T(8,128)(2,1)S(1)}, bf16[1024,1152]{1,0:T(8,128)(2,1)}, u32[]{:S(2)}) copy-start(bf16[1024,1152]{1,0:T(8,128)(2,1)} %param.8) | copy-start | bytes 7077892
  7.2 62.6 %all-gather.3.cloned.1.call-start = ((), (), s32[]{:S(2)}) async-start(), calls=%async_computation.2 | async-start | bytes 2654208 | tf_op jit(solution)/shard_map/all_gather | solution.py:20
  7.9 119.7 %all-gather.5.cloned.1.call-start = ((), (), s32[]{:S(2)}) async-start(), calls=%async_computation.4 | async-start | bytes 2654208 | tf_op jit(solution)/shard_map/all_gather | solution.py:44
  8.7 283.3 %all-reduce.3.cloned.1.call-start = ((), (), s32[]{:S(2)}) async-start(), calls=%async_computation.6 | async-start | bytes 25165824 | tf_op jit(solution)/shard_map/psum | solution.py:23
  69.7 5.5 %copy-start.5 = (bf16[1152,1024]{1,0:T(8,128)(2,1)S(1)}, bf16[1152,1024]{1,0:T(8,128)(2,1)}, u32[]{:S(2)}) copy-start(bf16[1152,1024]{1,0:T(8,128)(2,1)} %param.6) | copy-start | bytes 7077892
  69.7 5.5 %copy-start.7 = (bf16[1024,1152]{1,0:T(8,128)(2,1)S(1)}, bf16[1024,1152]{1,0:T(8,128)(2,1)}, u32[]{:S(2)}) copy-start(bf16[1024,1152]{1,0:T(8,128)(2,1)} %all-gather.3.cloned.1.call-done) | copy-start | bytes 7077892
  133.7 259.9 %reduce-scatter.3.cloned.1.call-start = ((), (), s32[]{:S(2)}) async-start(), calls=%async_computation.3 | async-start | bytes 5308416 | tf_op jit(solution)/shard_map/reduce_scatter | solution.py:38
  299.2 1.3 copy-start.2
  305.2 1.6 copy-start.3
  305.2 180.0 %reduce-scatter.5.cloned.1.call-start = ((), (), s32[]{:S(2)}) async-start(), calls=%async_computation.5 | async-start | bytes 5308416 | tf_op jit(solution)/shard_map/reduce_scatter | solution.py:49
  306.8 4.8 copy-start.4
  306.8 4.8 copy-start.6
  341.9 145.1 %copy-start.1 = (bf16[1024,1152]{1,0:T(8,128)(2,1)S(1)}, bf16[1024,1152]{1,0:T(8,128)(2,1)}, u32[]{:S(2)}) copy-start(bf16[1024,1152]{1,0:T(8,128)(2,1)} %param.8) | copy-start | bytes 7077892
Sparse Core Ops, SparseCore 0:
  10.3 59.3 all-gather.2
  72.0 55.5 all-gather.4
  133.9 158.0 all-reduce.2
  305.3 88.2 reduce-scatter.2
  398.0 87.1 reduce-scatter.4
where the time goes:
time: 494 us
  waiting for transfers between devices  400 us (81%)
  matrix products  49.6 us (10%)
  other arithmetic  15 us (3%)
  local copies, waits for them, and re-layouts  14.8 us (3%)
  between operations  13.8 us (3%)
    psum x1, waiting for transfers between devices, on_device(): lax.psum(jnp.concatenate([jnp.dot(block, gate_weight, preferred_element_t...  158 us
    reduce_scatter x1, waiting for transfers between devices, on_device(): lax.psum_scatter(times_transposed(grad_gate_pre, gate_weight) + times_tra...  89.7 us
    all_gather x1, waiting for transfers between devices, on_device(): rows_all = lax.all_gather(tokens, 'mp', axis=0, tiled=True)  61 us
    all_gather x1, waiting for transfers between devices, on_device(): cot_all = lax.all_gather(cotangent, 'mp', axis=0, tiled=True)  45.4 us
    reduce_scatter x1, waiting for transfers between devices, on_device(): lax.psum_scatter(jnp.dot(block, down_weight, preferred_element_type=jnp.f...  44.1 us
    dot_general x3, matrix products, inner_rows(): lax.dot_general(left, right, (((0,), (0,)), ((), ())), preferred_element_...  21.1 us
    dot_general x3, matrix products, times_transposed(): lax.dot_general(left, right, (((1,), (1,)), ((), ())), preferred_element_...  15.6 us
    unnamed x18, local copies, waits for them, and re-layouts  14.8 us
  transfers between devices with their start and end apart: 5, of which 5 were waited for; matrix products, arithmetic and copies ran while one was open for 12% of the time, Pallas kernels for 0%

commit v1 on v0

v1 whole, which is shorter than its diff:
```python
import jax
import jax.numpy as jnp
from jax import lax
from jax.sharding import PartitionSpec as P


def times_transposed(left, right):
    return lax.dot_general(
        left, right, (((1,), (1,)), ((), ())), preferred_element_type=jnp.float32
    )


def inner_rows(left, right):
    return lax.dot_general(
        left, right, (((0,), (0,)), ((), ())), preferred_element_type=jnp.float32
    )


def scatter_sum(part, axis):
    return lax.psum_scatter(part, axis, scatter_dimension=0, tiled=True)


def gather(part, axis):
    return lax.all_gather(part, axis, axis=0, tiled=True)


def on_device(tokens, gate_weight, up_weight, down_weight, cotangent):
    rows_all = gather(tokens, "mp")
    cot_all = gather(cotangent, "mp")
    gate = scatter_sum(jnp.dot(rows_all, gate_weight, preferred_element_type=jnp.float32), "dp")
    up = scatter_sum(jnp.dot(rows_all, up_weight, preferred_element_type=jnp.float32), "dp")
    grad_hidden = scatter_sum(times_transposed(cot_all, down_weight), "dp")
    sigma = jax.nn.sigmoid(gate)
    hidden = (gate * sigma * up).astype(jnp.bfloat16)
    hidden = gather(hidden, "dp")
    mixed = scatter_sum(jnp.dot(hidden, down_weight, preferred_element_type=jnp.float32), "mp").astype(jnp.bfloat16)
    grad_gate_pre = (grad_hidden * up * sigma * (1.0 + gate * (1.0 - sigma))).astype(jnp.bfloat16)
    grad_up_pre = (grad_hidden * gate * sigma).astype(jnp.bfloat16)
    grad_gate_pre = gather(grad_gate_pre, "dp")
    grad_up_pre = gather(grad_up_pre, "dp")
    grad_tokens = scatter_sum(
        times_transposed(grad_gate_pre, gate_weight) + times_transposed(grad_up_pre, up_weight),
        "mp",
    ).astype(jnp.bfloat16)
    grad_gate = inner_rows(rows_all, grad_gate_pre)
    grad_up = inner_rows(rows_all, grad_up_pre)
    grad_down = inner_rows(hidden, cot_all)
    return (mixed, grad_tokens, grad_gate, grad_up, grad_down)


def solution(mesh):
    in_specs = (P("mp", "dp"), P("dp", "mp"), P("dp", "mp"), P("mp", "dp"), P("mp", "dp"))
    out_specs = (P("mp", "dp"), P("mp", "dp"), P("dp", "mp"), P("dp", "mp"), P("mp", "dp"))
    return jax.shard_map(
        on_device, mesh=mesh, in_specs=in_specs, out_specs=out_specs, check_vma=False
    )
```

time: 494 us -> 634 us (1.28)
  waiting for transfers between devices: 400 us -> 535 us
  matrix products: 49.6 us -> 63.7 us
  other arithmetic: 15 us -> 5.61 us
    reduce_scatter x2 -> x5, waiting for transfers between devices: 134 us -> 329 us  [scatter_sum(): return lax.psum_scatter(part, axis, scatter_dimension=0, tiled=True)]
    psum x1 -> x0, waiting for transfers between devices: 158 us -> none  [on_device(): lax.psum(jnp.concatenate([jnp.dot(block, gate_weight, preferred_element_t...]
    all_gather x2 -> x5, waiting for transfers between devices: 106 us -> 203 us  [gather(): return lax.all_gather(part, axis, axis=0, tiled=True)]
    dot_general x3, matrix products: 13 us -> 21.1 us  [the longest x1 7.26 us: on_device(): jnp.dot(rows_all, up_weight, preferred_element_type=jnp.float32)]
    unnamed x18 -> x10, local copies, waits for them, and re-layouts: 14.8 us -> 13.9 us
  transfers between devices with their start and end apart: 5 -> 10, of which waited for: 5 -> 10; matrix products, arithmetic and copies ran while one was open for 12% -> 12% of each run, Pallas kernels for 0% -> 0%
where the time goes in v1:
time: 634 us; the launch traced here: 633 us
  waiting for transfers between devices  535 us (84%)
  matrix products  63.7 us (10%)
  between operations  14.2 us (2%)
  local copies, waits for them, and re-layouts  13.9 us (2%)
    reduce_scatter x5, waiting for transfers between devices, scatter_sum(): return lax.psum_scatter(part, axis, scatter_dimension=0, tiled=True)  329 us
    all_gather x5, waiting for transfers between devices, gather(): return lax.all_gather(part, axis, axis=0, tiled=True)  203 us
    dot_general x3, matrix products, times_transposed(): lax.dot_general(left, right, (((1,), (1,)), ((), ())), preferred_element_...  21.6 us
    dot_general x3, matrix products, inner_rows(): lax.dot_general(left, right, (((0,), (0,)), ((), ())), preferred_element_...  21 us
    unnamed x10, local copies, waits for them, and re-layouts  13.9 us
  transfers between devices with their start and end apart: 10, of which 10 were waited for; matrix products, arithmetic and copies ran while one was open for 12% of the time, Pallas kernels for 0%

profile of v1, /device:TPU:0, one launch (start us, length us, event | category | flops | bytes accessed | tf_op | source)
XLA Modules:
  0.0 633.2 jit_solution(2289008779031125263)
XLA Ops:
  7.2 0.0 copy-start
  7.2 0.0 all-gather.10.cloned.1.call-start
  7.2 0.7 all-gather.10.cloned.1.call-update
  7.9 0.0 all-gather.6.cloned.1.call-start
  8.0 0.7 all-gather.6.cloned.1.call-update
  8.7 0.0 reduce-scatter.12.cloned.1.call-start
  8.7 61.0 %all-gather.10.cloned.1.call-done = bf16[1024,1152]{1,0:T(8,128)(2,1)} async-done(((bf16[128,1152]{1,0:T(8,128)(2,1)}), bf16[1024,1152]{1,0:T(8,128)(2,1)}) %all-gather.10.cloned.1.call-update) | async-done | bytes 2359312 | tf_op jit(solution)/shard_map/all_gather | solution.py:24
  69.7 0.0 copy-done
  69.7 6.1 fusion.3
  75.8 0.0 reduce-scatter.12.cloned.1.call-update
  75.9 0.0 reduce-scatter.6.cloned.1.call-start
  75.9 51.7 %all-gather.6.cloned.1.call-done = bf16[1024,1152]{1,0:T(8,128)(2,1)} async-done(((bf16[128,1152]{1,0:T(8,128)(2,1)}), bf16[1024,1152]{1,0:T(8,128)(2,1)}) %all-gather.6.cloned.1.call-update) | async-done | bytes 2359312 | tf_op jit(solution)/shard_map/all_gather | solution.py:24
  127.6 7.3 %fusion = f32[1024,1024]{1,0:T(8,128)} fusion(bf16[1024,1152]{1,0:T(8,128)(2,1)} %all-gather.6.cloned.1.call-done, bf16[1152,1024]{1,0:T(8,128)(2,1)} %param.6), kind=kOutput, calls=%fused_computation.7 | convolution fusion | flops 2415919104 | bytes 8912896 | tf_op jit(solution)/shard_map/dot_general | solution.py:30
  134.9 0.0 reduce-scatter.6.cloned.1.call-update
  134.9 0.0 reduce-scatter.8.cloned.1.call-start
  134.9 7.3 %fusion.1 = f32[1024,1024]{1,0:T(8,128)} fusion(bf16[1024,1152]{1,0:T(8,128)(2,1)} %all-gather.6.cloned.1.call-done, bf16[1152,1024]{1,0:T(8,128)(2,1)} %param.7), kind=kOutput, calls=%fused_computation.8 | convolution fusion | flops 2415919104 | bytes 8912896 | tf_op jit(solution)/shard_map/dot_general | solution.py:31
  142.2 0.0 reduce-scatter.8.cloned.1.call-update
  142.2 0.0 all-gather.8.cloned.1.call-start
  142.3 53.9 %reduce-scatter.12.cloned.1.call-done = f32[64,1024]{1,0:T(8,128)} async-done(((f32[1024,1024]{1,0:T(8,128)}), f32[64,1024]{1,0:T(8,128)}) %reduce-scatter.12.cloned.1.call-update) | async-done | bytes 262160 | tf_op jit(solution)/shard_map/reduce_scatter | solution.py:20
  196.2 68.3 %reduce-scatter.6.cloned.1.call-done = f32[64,1024]{1,0:T(8,128)} async-done(((f32[1024,1024]{1,0:T(8,128)}), f32[64,1024]{1,0:T(8,128)}) %reduce-scatter.6.cloned.1.call-update) | async-done | bytes 262160 | tf_op jit(solution)/shard_map/reduce_scatter | solution.py:20
  264.5 68.3 %reduce-scatter.8.cloned.1.call-done = f32[64,1024]{1,0:T(8,128)} async-done(((f32[1024,1024]{1,0:T(8,128)}), f32[64,1024]{1,0:T(8,128)}) %reduce-scatter.8.cloned.1.call-update) | async-done | bytes 262160 | tf_op jit(solution)/shard_map/reduce_scatter | solution.py:20
  332.8 2.0 multiply_convert_fusion
  334.8 0.0 all-gather.8.cloned.1.call-update
  334.8 0.0 all-gather.12.cloned.1.call-start
  334.9 0.7 all-gather.12.cloned.1.call-update
  335.6 0.0 all-gather.14.cloned.1.call-start
  335.6 0.7 all-gather.14.cloned.1.call-update
  336.3 0.0 reduce-scatter.10.cloned.1.call-start
  336.4 31.1 %all-gather.8.cloned.1.call-done = bf16[1024,1024]{1,0:T(8,128)(2,1)} async-done(((bf16[64,1024]{1,0:T(8,128)(2,1)}), bf16[1024,1024]{1,0:T(8,128)(2,1)}) %all-gather.8.cloned.1.call-update) | async-done | bytes 2097168 | tf_op jit(solution)/shard_map/all_gather | solution.py:24
  367.4 6.6 %fusion.2 = f32[1024,1152]{1,0:T(8,128)} fusion(bf16[1024,1024]{1,0:T(8,128)(2,1)} %all-gather.8.cloned.1.call-done, bf16[1024,1152]{1,0:T(8,128)(2,1)S(1)} %copy-done), kind=kOutput, calls=%fused_computation.9 | convolution fusion | flops 2415919104 | bytes 9175040 | tf_op jit(solution)/shard_map/dot_general | solution.py:36
  374.0 0.0 reduce-scatter.10.cloned.1.call-update
  374.0 0.2 reduce-scatter.14.cloned.1.call-start
  374.3 29.5 %all-gather.12.cloned.1.call-done = bf16[1024,1024]{1,0:T(8,128)(2,1)} async-done(((bf16[64,1024]{1,0:T(8,128)(2,1)}), bf16[1024,1024]{1,0:T(8,128)(2,1)}) %all-gather.12.cloned.1.call-update) | async-done | bytes 2097168 | tf_op jit(solution)/shard_map/all_gather | solution.py:24
  403.8 0.0 copy-done.2
  403.8 6.7 %fusion.4 = f32[1024,1152]{1,0:T(8,128)} fusion(bf16[1024,1024]{1,0:T(8,128)(2,1)} %all-gather.12.cloned.1.call-done, bf16[1152,1024]{1,0:T(8,128)(2,1)S(1)} %copy-done.2), kind=kOutput, calls=%fused_computation.11 | convolution fusion | flops 2415919104 | bytes 9175040 | tf_op jit(solution)/shard_map/dot_general | solution.py:8
  410.5 29.7 %all-gather.14.cloned.1.call-done = bf16[1024,1024]{1,0:T(8,128)(2,1)} async-done(((bf16[64,1024]{1,0:T(8,128)(2,1)}), bf16[1024,1024]{1,0:T(8,128)(2,1)}) %all-gather.14.cloned.1.call-update) | async-done | bytes 2097168 | tf_op jit(solution)/shard_map/all_gather | solution.py:24
  440.1 8.8 %convolution_add_fusion = f32[1024,1152]{1,0:T(8,128)} fusion(f32[1024,1152]{1,0:T(8,128)} %fusion.4, bf16[1024,1024]{1,0:T(8,128)(2,1)} %all-gather.14.cloned.1.call-done, bf16[1152,1024]{1,0:T(8,128)(2,1)} %param.7), kind=kOutput, calls=%fused_computation | convolution fusion | flops 2417098752 | bytes 13893632 | tf_op jit(solution)/shard_map/dot_general | solution.py:8
  448.9 0.0 reduce-scatter.14.cloned.1.call-update
  449.0 1.6 copy-done.3
  450.6 6.7 %convolution_bitcast_fusion.1 = f32[1152,1024]{0,1:T(8,128)} fusion(bf16[1024,1024]{1,0:T(8,128)(2,1)} %all-gather.12.cloned.1.call-done, bf16[1024,1152]{1,0:T(8,128)(2,1)S(1)} %copy-done.3), kind=kOutput, calls=%fused_computation.2 | convolution fusion | flops 2415919104 | bytes 9175040 | tf_op jit(solution)/shard_map/dot_general | solution.py:14
  457.3 6.0 copy.10
  463.4 6.7 %convolution_bitcast_fusion = f32[1152,1024]{0,1:T(8,128)} fusion(bf16[1024,1024]{1,0:T(8,128)(2,1)} %all-gather.14.cloned.1.call-done, bf16[1024,1152]{1,0:T(8,128)(2,1)S(1)} %copy-done.3), kind=kOutput, calls=%fused_computation.1 | convolution fusion | flops 2415919104 | bytes 9175040 | tf_op jit(solution)/shard_map/dot_general | solution.py:14
  470.1 6.2 copy.11
  476.3 7.6 %fusion.5 = f32[1024,1152]{1,0:T(8,128)} fusion(bf16[1024,1024]{1,0:T(8,128)(2,1)} %all-gather.8.cloned.1.call-done, bf16[1024,1152]{1,0:T(8,128)(2,1)} %all-gather.10.cloned.1.call-done), kind=kOutput, calls=%fused_computation.12 | convolution fusion | flops 2415919104 | bytes 9175040 | tf_op jit(solution)/shard_map/dot_general | solution.py:14
  483.9 48.9 %reduce-scatter.10.cloned.1.call-done = f32[128,1152]{1,0:T(8,128)} async-done(((f32[1024,1152]{1,0:T(8,128)}), f32[128,1152]{1,0:T(8,128)}) %reduce-scatter.10.cloned.1.call-update) | async-done | bytes 589840 | tf_op jit(solution)/shard_map/reduce_scatter | solution.py:20
  532.8 1.8 convert_element_type.16
  534.6 90.0 %reduce-scatter.14.cloned.1.call-done = f32[128,1152]{1,0:T(8,128)} async-done(((f32[1024,1152]{1,0:T(8,128)}), f32[128,1152]{1,0:T(8,128)}) %reduce-scatter.14.cloned.1.call-update) | async-done | bytes 589840 | tf_op jit(solution)/shard_map/reduce_scatter | solution.py:20
  624.6 1.8 convert_element_type.19
  (4 shorter events, 0.0 us)
Async XLA Ops:
  7.2 62.6 %copy-start = (bf16[1024,1152]{1,0:T(8,128)(2,1)S(1)}, bf16[1024,1152]{1,0:T(8,128)(2,1)}, u32[]{:S(2)}) copy-start(bf16[1024,1152]{1,0:T(8,128)(2,1)} %param.8) | copy-start | bytes 7077892
  7.2 62.6 %all-gather.10.cloned.1.call-start = ((), (), s32[]{:S(2)}) async-start(), calls=%async_computation.10 | async-start | bytes 2654208 | tf_op jit(solution)/shard_map/all_gather | solution.py:24
  7.9 119.7 %all-gather.6.cloned.1.call-start = ((), (), s32[]{:S(2)}) async-start(), calls=%async_computation.5 | async-start | bytes 2654208 | tf_op jit(solution)/shard_map/all_gather | solution.py:24
  8.7 187.5 %reduce-scatter.12.cloned.1.call-start = ((), (), s32[]{:S(2)}) async-start(), calls=%async_computation.11 | async-start | bytes 4456448 | tf_op jit(solution)/shard_map/reduce_scatter | solution.py:20
  75.9 188.7 %reduce-scatter.6.cloned.1.call-start = ((), (), s32[]{:S(2)}) async-start(), calls=%async_computation.6 | async-start | bytes 4456448 | tf_op jit(solution)/shard_map/reduce_scatter | solution.py:20
  134.9 197.9 %reduce-scatter.8.cloned.1.call-start = ((), (), s32[]{:S(2)}) async-start(), calls=%async_computation.7 | async-start | bytes 4456448 | tf_op jit(solution)/shard_map/reduce_scatter | solution.py:20
  142.2 225.2 %all-gather.8.cloned.1.call-start = ((), (), s32[]{:S(2)}) async-start(), calls=%async_computation.8 | async-start | bytes 2228224 | tf_op jit(solution)/shard_map/all_gather | solution.py:24
  334.8 69.0 %all-gather.12.cloned.1.call-start = ((), (), s32[]{:S(2)}) async-start(), calls=%async_computation.12 | async-start | bytes 2228224 | tf_op jit(solution)/shard_map/all_gather | solution.py:24
  335.6 104.6 %all-gather.14.cloned.1.call-start = ((), (), s32[]{:S(2)}) async-start(), calls=%async_computation.13 | async-start | bytes 2228224 | tf_op jit(solution)/shard_map/all_gather | solution.py:24
  336.3 196.4 %reduce-scatter.10.cloned.1.call-start = ((), (), s32[]{:S(2)}) async-start(), calls=%async_computation.9 | async-start | bytes 5308416 | tf_op jit(solution)/shard_map/reduce_scatter | solution.py:20
  374.0 29.8 %copy-start.2 = (bf16[1152,1024]{1,0:T(8,128)(2,1)S(1)}, bf16[1152,1024]{1,0:T(8,128)(2,1)}, u32[]{:S(2)}) copy-start(bf16[1152,1024]{1,0:T(8,128)(2,1)} %param.6) | copy-start | bytes 7077892
  374.0 250.5 %reduce-scatter.14.cloned.1.call-start = ((), (), s32[]{:S(2)}) async-start(), calls=%async_computation.14 | async-start | bytes 5308416 | tf_op jit(solution)/shard_map/reduce_scatter | solution.py:20
  448.9 1.7 copy-start.3
  476.3 150.1 %copy-start.1 = (bf16[1024,1152]{1,0:T(8,128)(2,1)S(1)}, bf16[1024,1152]{1,0:T(8,128)(2,1)}, u32[]{:S(2)}) copy-start(bf16[1024,1152]{1,0:T(8,128)(2,1)} %param.8) | copy-start | bytes 7077892
Sparse Core Ops, SparseCore 0:
  10.3 59.3 all-gather.9
  72.0 55.5 all-gather.5
  130.6 65.5 reduce-scatter.11
  199.0 65.4 reduce-scatter.5
  267.3 65.4 reduce-scatter.7
  335.0 32.4 all-gather.7
  369.7 34.0 all-gather.11
  406.1 34.0 all-gather.13
  444.1 88.6 reduce-scatter.9
  537.1 87.4 reduce-scatter.13

commit v2 on v1

v2 whole, which is shorter than its diff:
```python
import functools

import jax
import jax.numpy as jnp
from jax import lax
from jax.experimental import pallas as pl
from jax.experimental.pallas import tpu as pltpu
from jax.sharding import PartitionSpec as P

MESH = pl.DeviceIdType.MESH
F32 = jnp.float32
BF16 = jnp.bfloat16
CHUNKS = 4
Y, X = 4, 4


def dot(left, right):
    return lax.dot_general(left, right, (((1,), (0,)), ((), ())), preferred_element_type=F32)


def dot_t(left, right):
    return lax.dot_general(left, right, (((1,), (1,)), ((), ())), preferred_element_type=F32)


def inner_rows(left, right):
    return lax.dot_general(left, right, (((0,), (0,)), ((), ())), preferred_element_type=F32)


COLUMNS = {}
for name, copies in (
    ("tok_z", 1), ("cot_y", 3), ("tok_y", 3), ("cot_z", 1),
    ("core0", 1), ("core1", 1), ("x0", 3), ("x1", 3), ("z0", 1), ("z1", 1),
    ("back_z0", 1), ("back_z1", 1), ("back_x0", 3), ("back_x1", 3), ("back_c0", 1), ("back_c1", 1),
    ("mix_y", 3), ("mix_z", 1), ("gt_z", 1), ("gt_y", 3),
):
    COLUMNS[name] = (sum(n for _, n in COLUMNS.values()), copies)
TOTAL = sum(n for _, n in COLUMNS.values())


def kernel(
    tokens, gate_w, up_w, down_w, cotangent,
    mixed, grad_tokens, tok_out, cot_out, hid_out, ggp_out, gup_out,
    gw, uw, dw, tok, cot, part, crecv, xs, xr, xown, zr, full, tmp,
    ms, mown, mr, mz, mzr, gs, gown, gr, gys, gyr,
    send_sem, recv_sem, load_sem, own_sem, out_sem,
):
    rows = 128 // CHUNKS
    height = 1024 // CHUNKS
    share = height // 16
    dp, mp = lax.axis_index("dp"), lax.axis_index("mp")
    core = lax.rem(dp, 2)
    x = lax.rem(dp // 2, 4)
    zl = dp // 8
    y = mp // 2
    zh = lax.rem(mp, 2)

    def at_x(k):
        return (zl * 8 + lax.rem(x + k, 4) * 2 + core, mp)

    def at_y(k):
        return (dp, lax.rem(y + k, 4) * 2 + zh)

    at_core = (dp + 1 - 2 * core, mp)
    at_zl = (lax.rem(dp + 8, 16), mp)
    at_zh = (dp, mp + 1 - 2 * zh)

    def remote(name, q, j, src, dst, target):
        column = COLUMNS[name][0] + j
        return pltpu.make_async_remote_copy(
            src_ref=src, dst_ref=dst,
            send_sem=send_sem.at[q, column], recv_sem=recv_sem.at[q, column],
            device_id=target, device_id_type=MESH,
        )

    def mine(q):
        return pl.ds(pl.multiple_of(q * rows, rows), rows)

    def chunk_rows(q):
        return pl.ds(pl.multiple_of(q * height, height), height)

    GROUP = (slice(0, 2), slice(2, 3))
    BACK = (slice(0, 1), slice(1, 3))

    def copies(name, q):
        kind, g = name[:-1], None
        if name[-1] in "01":
            g = int(name[-1])
        if name == "tok_z":
            return [remote(name, q, 0, tokens.at[mine(q)], tok.at[q, y, zh], at_zh)]
        if name == "cot_y":
            return [remote(name, q, k - 1, cotangent.at[mine(q)], cot.at[q, y, zh], at_y(k)) for k in (1, 3, 2)]
        if name == "tok_y":
            return [remote(name, q, k - 1, tok.at[q, y], tok.at[q, y], at_y(k)) for k in (1, 3, 2)]
        if name == "cot_z":
            return [remote(name, q, 0, cot.at[q, :, zh], cot.at[q, :, zh], at_zh)]
        if kind == "core":
            return [remote(name, q, 0, part.at[lax.rem(q, 2), GROUP[g], 1 - core], crecv.at[q, GROUP[g]], at_core)]
        if kind == "x":
            return [remote(name, q, k - 1, xs.at[q, GROUP[g], lax.rem(x + k, 4)], xr.at[q, k - 1, GROUP[g]], at_x(k)) for k in (1, 3, 2)]
        if kind == "z":
            return [remote(name, q, 0, xown.at[q, GROUP[g], 1 - zl], zr.at[q, GROUP[g]], at_zl)]
        if kind == "back_z":
            ref = full.at[q, BACK[g], core, x, zl]
            return [remote(name, q, 0, ref, ref, at_zl)]
        if kind == "back_x":
            ref = full.at[q, BACK[g], core, x]
            return [remote(name, q, k - 1, ref, ref, at_x(k)) for k in (1, 3, 2)]
        if kind == "back_c":
            ref = full.at[q, BACK[g], core]
            return [remote(name, q, 0, ref, ref, at_core)]
        if name == "mix_y":
            return [remote(name, q, k - 1, ms.at[q, lax.rem(y + k, 4)], mr.at[q, k - 1], at_y(k)) for k in (1, 3, 2)]
        if name == "mix_z":
            return [remote(name, q, 0, mz.at[q], mzr.at[q], at_zh)]
        if name == "gt_z":
            return [remote(name, q, 0, gs.at[q, :, 1 - zh], gr.at[q], at_zh)]
        if name == "gt_y":
            return [remote(name, q, k - 1, gys.at[q, lax.rem(y + k, 4)], gyr.at[q, k - 1], at_y(k)) for k in (1, 3, 2)]

    def start(name, q):
        for copy in copies(name, q):
            copy.start()

    def arrived(name, q):
        for copy in copies(name, q):
            copy.wait_recv()

    def sent(name, q):
        for copy in copies(name, q):
            copy.wait_send()

    def own_copies(q):
        return [
            pltpu.make_async_copy(tokens.at[mine(q)], tok.at[q, y, zh], own_sem.at[q, 0]),
            pltpu.make_async_copy(cotangent.at[mine(q)], cot.at[q, y, zh], own_sem.at[q, 1]),
        ]

    loads = [
        pltpu.make_async_copy(gate_w, gw, load_sem.at[0]),
        pltpu.make_async_copy(up_w, uw, load_sem.at[1]),
        pltpu.make_async_copy(down_w, dw, load_sem.at[2]),
    ]

    def out_copy(q, i):
        src = (tok.at[q], cot.at[q], full.at[q, 0], full.at[q, 1], full.at[q, 2])[i]
        dst = (tok_out, cot_out, hid_out, ggp_out, gup_out)[i].at[q]
        return pltpu.make_async_copy(src, dst, out_sem.at[q, i])

    def a0(q):
        start("tok_z", q)
        start("cot_y", q)

    def a1(q):
        for copy in own_copies(q):
            copy.wait()
        arrived("tok_z", q)
        start("tok_y", q)
        arrived("cot_y", q)
        start("cot_z", q)

    def g1a(q):
        arrived("tok_y", q)
        out_copy(q, 0).start()
        block = tok[q].reshape(height, 1152)
        slot = lax.rem(q, 2)

        @pl.loop(0, 4)
        def _(n):
            cols = pl.ds(pl.multiple_of(n * 256, 256), 256)
            part[slot, 0, :, :, cols] = dot(block, gw[:, cols]).reshape(2, height // 2, 256)
            part[slot, 1, :, :, cols] = dot(block, uw[:, cols]).reshape(2, height // 2, 256)

        start("core0", q)

    def g1b(q):
        arrived("cot_z", q)
        out_copy(q, 1).start()
        block = cot[q].reshape(height, 1152)
        slot = lax.rem(q, 2)

        @pl.loop(0, 4)
        def _(n):
            cols = pl.ds(pl.multiple_of(n * 256, 256), 256)
            part[slot, 2, :, :, cols] = dot_t(block, dw[cols, :]).reshape(2, height // 2, 256)

        start("core1", q)

    def b1(q, g):
        arrived(f"core{g}", q)
        sent(f"core{g}", q)
        slot = lax.rem(q, 2)
        for i in range(*((0, 2), (2, 3))[g]):
            total = part[slot, i, core] + crecv[q, i]
            part[slot, i, core] = total
            xs[q, i] = total.astype(BF16).reshape(4, 2, share, 1024)
            own = pl.ds(pl.multiple_of(x * 2 * share, 2 * share), 2 * share)
            xown[q, i] = part[slot, i, core, own].reshape(2, share, 1024)
        start(f"x{g}", q)

    def b2(q, g):
        arrived(f"x{g}", q)
        for i in range(*((0, 2), (2, 3))[g]):
            xown[q, i] = (
                xown[q, i] + xr[q, 0, i].astype(F32) + xr[q, 1, i].astype(F32) + xr[q, 2, i].astype(F32)
            )
        start(f"z{g}", q)

    def e_a(q):
        arrived("z0", q)
        gate = xown[q, 0, zl] + zr[q, 0]
        up = xown[q, 1, zl] + zr[q, 1]
        zr[q, 0] = gate
        zr[q, 1] = up
        sigma = jax.nn.sigmoid(gate)
        full[q, 0, core, x, zl] = (gate * sigma * up).astype(BF16)
        start("back_z0", q)

    def e_b(q):
        arrived("z1", q)
        gate = zr[q, 0]
        up = zr[q, 1]
        sigma = jax.nn.sigmoid(gate)
        grad = xown[q, 2, zl] + zr[q, 2]
        full[q, 1, core, x, zl] = (grad * up * sigma * (1.0 + gate * (1.0 - sigma))).astype(BF16)
        full[q, 2, core, x, zl] = (grad * gate * sigma).astype(BF16)
        start("back_z1", q)

    def c1(q, g):
        arrived(f"back_z{g}", q)
        start(f"back_x{g}", q)

    def c2(q, g):
        arrived(f"back_x{g}", q)
        start(f"back_c{g}", q)

    def g2a(q):
        arrived("back_c0", q)
        out_copy(q, 2).start()
        block = full[q, 0].reshape(height, 1024)

        @pl.loop(0, 3)
        def _(n):
            cols = pl.ds(pl.multiple_of(n * 384, 384), 384)
            tmp[:, :, :, cols] = dot(block, dw[:, cols]).reshape(4, 2, rows, 384)

        ms[q] = tmp[...].astype(BF16)
        mown[q] = tmp[y]
        start("mix_y", q)

    def g2b(q):
        arrived("back_c1", q)
        out_copy(q, 3).start()
        out_copy(q, 4).start()
        left = full[q, 1].reshape(height, 1024)
        right = full[q, 2].reshape(height, 1024)

        @pl.loop(0, 3)
        def _(n):
            cols = pl.ds(pl.multiple_of(n * 384, 384), 384)
            tmp[:, :, :, cols] = (dot_t(left, gw[cols, :]) + dot_t(right, uw[cols, :])).reshape(4, 2, rows, 384)

        gs[q] = tmp[...].astype(BF16)
        gown[q] = tmp[:, zh]
        start("gt_z", q)

    def d1a(q):
        arrived("mix_y", q)
        mown[q] = mown[q] + mr[q, 0].astype(F32) + mr[q, 1].astype(F32) + mr[q, 2].astype(F32)
        mz[q] = mown[q, 1 - zh].astype(BF16)
        start("mix_z", q)

    def d1b(q):
        arrived("gt_z", q)
        total = gown[q] + gr[q].astype(F32)
        gown[q] = total
        gys[q] = total.astype(BF16)
        start("gt_y", q)

    def d2a(q):
        arrived("mix_z", q)
        mixed[mine(q), :] = (mown[q, zh] + mzr[q].astype(F32)).astype(BF16)

    def d2b(q):
        arrived("gt_y", q)
        grad_tokens[mine(q), :] = (
            gown[q, y] + gyr[q, 0].astype(F32) + gyr[q, 1].astype(F32) + gyr[q, 2].astype(F32)
        ).astype(BF16)

    for copy in loads:
        copy.start()
    peers = [at_core, at_zl, at_zh] + [at_x(k) for k in (1, 2, 3)] + [at_y(k) for k in (1, 2, 3)]
    barrier = pltpu.get_barrier_semaphore()
    for peer in peers:
        pl.semaphore_signal(barrier, inc=1, device_id=peer, device_id_type=MESH)
    for q in range(CHUNKS):
        for copy in own_copies(q):
            copy.start()
    pl.semaphore_wait(barrier, len(peers))
    a0(0)
    for copy in loads:
        copy.wait()

    plan = PLAN(locals())
    ticks = CHUNKS + max(delay for _, delay in plan)

    @pl.loop(0, ticks)
    def _(t):
        for stage, delay in plan:
            q = t - delay

            @pl.when(jnp.logical_and(q >= 0, q < CHUNKS))
            def _():
                stage(q)

    @pl.loop(0, CHUNKS)
    def _(q):
        for name in COLUMNS:
            if not name.startswith("core"):
                sent(name, q)
        for i in range(5):
            out_copy(q, i).wait()


def PLAN(s):
    b1, b2, c1, c2 = s["b1"], s["b2"], s["c1"], s["c2"]

    def next_a0(q):
        @pl.when(q + 1 < CHUNKS)
        def _():
            s["a0"](q + 1)

    return [
        (s["e_a"], 2), (s["e_b"], 2),
        (lambda q: b1(q, 0), 1), (lambda q: b1(q, 1), 1),
        (s["g2a"], 3), (s["g2b"], 3),
        (lambda q: c1(q, 0), 2), (lambda q: c1(q, 1), 2),
        (s["a1"], 0), (next_a0, 0),
        (lambda q: b2(q, 0), 1), (lambda q: b2(q, 1), 1),
        (s["d1a"], 3), (s["d1b"], 3),
        (s["g1a"], 0), (s["g1b"], 0),
        (lambda q: c2(q, 0), 2), (lambda q: c2(q, 1), 2),
        (s["d2a"], 3), (s["d2b"], 3),
    ]


def block(tokens, gate_weight, up_weight, down_weight, cotangent):
    n = CHUNKS
    rows, height = 128 // n, 1024 // n
    share = height // 16
    anyspace = pl.BlockSpec(memory_space=pl.ANY)
    vmem = pl.BlockSpec(memory_space=pltpu.VMEM)
    out_shape = [
        jax.ShapeDtypeStruct((128, 1152), BF16),
        jax.ShapeDtypeStruct((128, 1152), BF16),
        jax.ShapeDtypeStruct((n, Y, 2, rows, 1152), BF16),
        jax.ShapeDtypeStruct((n, Y, 2, rows, 1152), BF16),
        jax.ShapeDtypeStruct((n, 2, X, 2, share, 1024), BF16),
        jax.ShapeDtypeStruct((n, 2, X, 2, share, 1024), BF16),
        jax.ShapeDtypeStruct((n, 2, X, 2, share, 1024), BF16),
    ]
    V = pltpu.VMEM
    scratch = [
        V((1152, 1024), BF16), V((1152, 1024), BF16), V((1024, 1152), BF16),
        V((n, Y, 2, rows, 1152), BF16), V((n, Y, 2, rows, 1152), BF16),
        V((2, 3, 2, height // 2, 1024), F32), V((n, 3, height // 2, 1024), F32),
        V((n, 3, X, 2, share, 1024), BF16), V((n, 3, 3, 2, share, 1024), BF16),
        V((n, 3, 2, share, 1024), F32), V((n, 3, share, 1024), F32),
        V((n, 3, 2, X, 2, share, 1024), BF16),
        V((Y, 2, rows, 1152), F32),
        V((n, Y, 2, rows, 1152), BF16), V((n, 2, rows, 1152), F32), V((n, 3, 2, rows, 1152), BF16),
        V((n, rows, 1152), BF16), V((n, rows, 1152), BF16),
        V((n, Y, 2, rows, 1152), BF16), V((n, Y, rows, 1152), F32), V((n, Y, rows, 1152), BF16),
        V((n, Y, rows, 1152), BF16), V((n, 3, rows, 1152), BF16),
        pltpu.SemaphoreType.DMA((n, TOTAL)), pltpu.SemaphoreType.DMA((n, TOTAL)),
        pltpu.SemaphoreType.DMA((3,)), pltpu.SemaphoreType.DMA((n, 2)), pltpu.SemaphoreType.DMA((n, 5)),
    ]
    return pl.pallas_call(
        kernel,
        out_shape=out_shape,
        in_specs=[anyspace] * 5,
        out_specs=[vmem, vmem] + [anyspace] * 5,
        scratch_shapes=scratch,
        compiler_params=pltpu.CompilerParams(
            collective_id=0, has_side_effects=True, vmem_limit_bytes=62 << 20
        ),
        cost_estimate=pl.CostEstimate(flops=14_500_000_000, bytes_accessed=30_000_000, transcendentals=0),
        name="exchange",
    )(tokens, gate_weight, up_weight, down_weight, cotangent)


def on_device(tokens, gate_weight, up_weight, down_weight, cotangent):
    mixed, grad_tokens, rows_all, cot_all, hidden, ggp, gup = block(
        tokens, gate_weight, up_weight, down_weight, cotangent
    )
    rows_all = rows_all.reshape(1024, 1152)
    cot_all = cot_all.reshape(1024, 1152)
    hidden, ggp, gup = (a.reshape(1024, 1024) for a in (hidden, ggp, gup))
    grad_gate = inner_rows(rows_all, ggp)
    grad_up = inner_rows(rows_all, gup)
    grad_down = inner_rows(hidden, cot_all)
    return (mixed, grad_tokens, grad_gate, grad_up, grad_down)


def solution(mesh):
    in_specs = (P("mp", "dp"), P("dp", "mp"), P("dp", "mp"), P("mp", "dp"), P("mp", "dp"))
    out_specs = (P("mp", "dp"), P("mp", "dp"), P("dp", "mp"), P("dp", "mp"), P("mp", "dp"))
    return jax.shard_map(
        on_device, mesh=mesh, in_specs=in_specs, out_specs=out_specs, check_vma=False
    )
```

time: 634 us -> 164 us (0.26)
  waiting for transfers between devices: 535 us -> 0 us
  Pallas kernels: 0 us -> 145 us
  matrix products: 63.7 us -> 16.2 us
  between operations: 14.2 us -> 0.68 us
  local copies, waits for them, and re-layouts: 13.9 us -> 1.45 us
    reduce_scatter x5 -> x0, waiting for transfers between devices: 329 us -> none  [scatter_sum(): return lax.psum_scatter(part, axis, scatter_dimension=0, tiled=True)]
    all_gather x5 -> x0, waiting for transfers between devices: 203 us -> none  [gather(): return lax.all_gather(part, axis, axis=0, tiled=True)]
    pallas_call x0 -> x1, Pallas kernels: none -> 145 us  [block(): pl.pallas_call(kernel, out_shape=out_shape, in_specs=[anyspace] * 5, out_...]
    dot_general x6 -> x0, matrix products: 42.7 us -> none  [the longest x3 21.6 us: times_transposed(): lax.dot_general(left, right, (((1,), (1,)), ((), ())), preferred_element_...]
    unnamed x10 -> x14, local copies, waits for them, and re-layouts: 13.9 us -> 1.45 us
  transfers between devices with their start and end apart: 10 -> 0, of which waited for: 10 -> 0; matrix products, arithmetic and copies ran while one was open for 12% -> 0% of each run, Pallas kernels for 0% -> 0%
where the time goes in v2:
time: 164 us
  Pallas kernels  145 us (88%)
  matrix products  16.2 us (10%)
    pallas_call x1, Pallas kernels, block(): pl.pallas_call(kernel, out_shape=out_shape, in_specs=[anyspace] * 5, out_...  145 us
    dot_general x3, matrix products, inner_rows(): lax.dot_general(left, right, (((0,), (0,)), ((), ())), preferred_element_...  16.2 us

profile of v2, /device:TPU:0, one launch (start us, length us, event | category | flops | bytes accessed | tf_op | source)
XLA Modules:
  0.0 163.7 jit_solution(16644119629878433395)
XLA Ops:
  0.6 145.4 %exchange.1 = (bf16[128,1152]{1,0:T(8,128)(2,1)}, bf16[128,1152]{1,0:T(8,128)(2,1)}, bf16[4,4,2,32,1152]{4,3,2,1,0:T(8,128)(2,1)}, bf16[4,4,2,32,1152]{4,3,2,1,0...) custom-call(bf16[128,1152]{1,0:T(8,128)(2,1)} %tokens.1, ...), custom_call_target="tpu_custom_call" | custom-call | flops 14499999744 | bytes 30000000 | tf_op jit(solution)/shard_map/exchange/pallas_call | solution.py:377
  146.1 0.0 copy-start.3
  146.1 0.0 copy-start.5
  146.1 7.3 %fusion.1 = f32[1152,1024]{1,0:T(8,128)} fusion(bf16[1024,1152]{1,0:T(8,128)(2,1)} %bitcast.12, bf16[1024,1024]{1,0:T(8,128)(2,1)} %bitcast.16), kind=kOutput, calls=%fused_computation.1 | convolution fusion | flops 2415919104 | bytes 9175040 | tf_op jit(solution)/shard_map/dot_general | solution.py:26
  153.4 0.0 copy-done.3
  153.4 0.0 copy-done.5
  153.4 0.0 copy-start.2
  153.4 0.0 copy-start.4
  153.4 4.3 %fusion = f32[1152,1024]{1,0:T(8,128)} fusion(bf16[1024,1152]{1,0:T(8,128)(2,1)S(1)} %bitcast.13, bf16[1024,1024]{1,0:T(8,128)(2,1)S(1)} %bitcast.15), kind=kOutput, calls=%fused_computation | convolution fusion | flops 2415919104 | bytes 9175040 | tf_op jit(solution)/shard_map/dot_general | solution.py:26
  157.7 0.0 copy-done.2
  157.7 0.0 copy-done.4
  157.7 0.0 copy-start.1
  157.7 0.0 copy-start
  157.7 4.6 %fusion.2 = f32[1024,1152]{1,0:T(8,128)} fusion(bf16[1024,1024]{1,0:T(8,128)(2,1)S(1)} %bitcast.14, bf16[1024,1152]{1,0:T(8,128)(2,1)S(1)} %bitcast.11), kind=kOutput, calls=%fused_computation.2 | convolution fusion | flops 2415919104 | bytes 9175040 | tf_op jit(solution)/shard_map/dot_general | solution.py:26
  162.3 0.0 copy-done.1
  162.3 0.7 copy.12
  163.0 0.0 copy-done
  163.0 0.7 copy.13
Async XLA Ops:
  146.1 7.3 %copy-start.3 = (bf16[4,4,2,32,1152]{4,3,2,1,0:T(8,128)(2,1)S(1)}, bf16[4,4,2,32,1152]{4,3,2,1,0:T(8,128)(2,1)}, u32[]{:S(2)}) copy-start(bf16[4,4,2,32,1152]{4,3,2,1,0:T(8,128)(2,1)} %get-tuple-element.14) | copy-start | bytes 7077892
  146.1 7.3 %copy-start.5 = (bf16[4,2,4,2,16,1024]{5,4,3,2,1,0:T(8,128)(2,1)S(1)}, bf16[4,2,4,2,16,1024]{5,4,3,2,1,0:T(8,128)(2,1)}, u32[]{:S(2)}) copy-start(bf16[4,2,4,2,16,1024]{5,4,3,2,1,0:T(8,128)(2,1)} %get-tuple-element.15) | copy-start | bytes 6291460
  153.4 4.3 %copy-start.2 = (bf16[4,4,2,32,1152]{4,3,2,1,0:T(8,128)(2,1)S(1)}, bf16[4,4,2,32,1152]{4,3,2,1,0:T(8,128)(2,1)}, u32[]{:S(2)}) copy-start(bf16[4,4,2,32,1152]{4,3,2,1,0:T(8,128)(2,1)} %get-tuple-element.18) | copy-start | bytes 7077892
  153.4 4.3 %copy-start.4 = (bf16[4,2,4,2,16,1024]{5,4,3,2,1,0:T(8,128)(2,1)S(1)}, bf16[4,2,4,2,16,1024]{5,4,3,2,1,0:T(8,128)(2,1)}, u32[]{:S(2)}) copy-start(bf16[4,2,4,2,16,1024]{5,4,3,2,1,0:T(8,128)(2,1)} %get-tuple-element.17) | copy-start | bytes 6291460
  157.7 4.6 %copy-start.1 = (bf16[128,1152]{1,0:T(8,128)(2,1)S(1)}, bf16[128,1152]{1,0:T(8,128)(2,1)}, u32[]{:S(2)}) copy-start(bf16[128,1152]{1,0:T(8,128)(2,1)} %get-tuple-element.24) | copy-start | bytes 884740
  157.7 5.4 %copy-start = (bf16[128,1152]{1,0:T(8,128)(2,1)S(1)}, bf16[128,1152]{1,0:T(8,128)(2,1)}, u32[]{:S(2)}) copy-start(bf16[128,1152]{1,0:T(8,128)(2,1)} %get-tuple-element.25) | copy-start | bytes 884740

commit v3 on v2

--- a/solution.py
+++ b/solution.py
@@ -30,7 +30,7 @@
 for name, copies in (
     ("tok_z", 1), ("cot_y", 3), ("tok_y", 3), ("cot_z", 1),
     ("core0", 1), ("core1", 1), ("x0", 3), ("x1", 3), ("z0", 1), ("z1", 1),
-    ("back_z0", 1), ("back_z1", 1), ("back_x0", 3), ("back_x1", 3), ("back_c0", 1), ("back_c1", 1),
+    ("back_x0", 2), ("back_x1", 2), ("pass_x0", 2), ("pass_x1", 2), ("back_c0", 1), ("back_c1", 1),
     ("mix_y", 3), ("mix_z", 1), ("gt_z", 1), ("gt_y", 3),
 ):
     COLUMNS[name] = (sum(n for _, n in COLUMNS.values()), copies)
@@ -40,13 +40,13 @@
 def kernel(
     tokens, gate_w, up_w, down_w, cotangent,
     mixed, grad_tokens, tok_out, cot_out, hid_out, ggp_out, gup_out,
-    gw, uw, dw, tok, cot, part, crecv, xs, xr, xown, zr, full, tmp,
+    gw, uw, dw, tok, cot, part, crecv, xs, xr, xown, zs, zr, full, tmp,
     ms, mown, mr, mz, mzr, gs, gown, gr, gys, gyr,
     send_sem, recv_sem, load_sem, own_sem, out_sem,
 ):
     rows = 128 // CHUNKS
     height = 1024 // CHUNKS
-    share = height // 16
+    share = height // 8
     dp, mp = lax.axis_index("dp"), lax.axis_index("mp")
     core = lax.rem(dp, 2)
     x = lax.rem(dp // 2, 4)
@@ -94,17 +94,20 @@
         if name == "cot_z":
             return [remote(name, q, 0, cot.at[q, :, zh], cot.at[q, :, zh], at_zh)]
         if kind == "core":
-            return [remote(name, q, 0, part.at[lax.rem(q, 2), GROUP[g], 1 - core], crecv.at[q, GROUP[g]], at_core)]
+            return [remote(name, q, 0, part.at[q, GROUP[g], 1 - core], crecv.at[q, GROUP[g]], at_core)]
         if kind == "x":
             return [remote(name, q, k - 1, xs.at[q, GROUP[g], lax.rem(x + k, 4)], xr.at[q, k - 1, GROUP[g]], at_x(k)) for k in (1, 3, 2)]
         if kind == "z":
-            return [remote(name, q, 0, xown.at[q, GROUP[g], 1 - zl], zr.at[q, GROUP[g]], at_zl)]
-        if kind == "back_z":
-            ref = full.at[q, BACK[g], core, x, zl]
-            return [remote(name, q, 0, ref, ref, at_zl)]
+            return [remote(name, q, 0, zs.at[q, GROUP[g]], zr.at[q, GROUP[g]], at_zl)]
         if kind == "back_x":
             ref = full.at[q, BACK[g], core, x]
-            return [remote(name, q, k - 1, ref, ref, at_x(k)) for k in (1, 3, 2)]
+            return [remote(name, q, i, ref, ref, at_x(k)) for i, k in enumerate((1, 3))]
+        if kind == "pass_x":
+            result = []
+            for i, k in enumerate((1, 3)):
+                ref = full.at[q, BACK[g], core, lax.rem(x + 4 - k, 4), :, pl.ds(i * 512, 512)]
+                result.append(remote(name, q, i, ref, ref, at_x(k)))
+            return result
         if kind == "back_c":
             ref = full.at[q, BACK[g], core]
             return [remote(name, q, 0, ref, ref, at_core)]
@@ -129,17 +132,13 @@
         for copy in copies(name, q):
             copy.wait_send()
 
-    def own_copies(q):
-        return [
-            pltpu.make_async_copy(tokens.at[mine(q)], tok.at[q, y, zh], own_sem.at[q, 0]),
-            pltpu.make_async_copy(cotangent.at[mine(q)], cot.at[q, y, zh], own_sem.at[q, 1]),
-        ]
-
-    loads = [
-        pltpu.make_async_copy(gate_w, gw, load_sem.at[0]),
-        pltpu.make_async_copy(up_w, uw, load_sem.at[1]),
-        pltpu.make_async_copy(down_w, dw, load_sem.at[2]),
-    ]
+    def own_copy(q, i):
+        src, dst = ((tokens, tok), (cotangent, cot))[i]
+        return pltpu.make_async_copy(src.at[mine(q)], dst.at[q, y, zh], own_sem.at[q, i])
+
+    def load(i):
+        src, dst = ((gate_w, gw), (up_w, uw), (down_w, dw))[i]
+        return pltpu.make_async_copy(src, dst, load_sem.at[i])
 
     def out_copy(q, i):
         src = (tok.at[q], cot.at[q], full.at[q, 0], full.at[q, 1], full.at[q, 2])[i]
@@ -150,19 +149,24 @@
         start("tok_z", q)
         start("cot_y", q)
 
-    def a1(q):
-        for copy in own_copies(q):
-            copy.wait()
+    def a1t(q):
+        own_copy(q, 0).wait()
         arrived("tok_z", q)
         start("tok_y", q)
+
+    def a1c(q):
+        own_copy(q, 1).wait()
         arrived("cot_y", q)
         start("cot_z", q)
 
     def g1a(q):
         arrived("tok_y", q)
+        if q == 0:
+            load(0).wait()
+            load(1).wait()
         out_copy(q, 0).start()
         block = tok[q].reshape(height, 1152)
-        slot = lax.rem(q, 2)
+        slot = q
 
         @pl.loop(0, 4)
         def _(n):
@@ -174,9 +178,11 @@
 
     def g1b(q):
         arrived("cot_z", q)
+        if q == 0:
+            load(2).wait()
         out_copy(q, 1).start()
         block = cot[q].reshape(height, 1152)
-        slot = lax.rem(q, 2)
+        slot = q
 
         @pl.loop(0, 4)
         def _(n):
@@ -188,49 +194,44 @@
     def b1(q, g):
         arrived(f"core{g}", q)
         sent(f"core{g}", q)
-        slot = lax.rem(q, 2)
         for i in range(*((0, 2), (2, 3))[g]):
-            total = part[slot, i, core] + crecv[q, i]
-            part[slot, i, core] = total
-            xs[q, i] = total.astype(BF16).reshape(4, 2, share, 1024)
-            own = pl.ds(pl.multiple_of(x * 2 * share, 2 * share), 2 * share)
-            xown[q, i] = part[slot, i, core, own].reshape(2, share, 1024)
+            total = part[q, i, core] + crecv[q, i]
+            xs[q, i] = total.astype(BF16).reshape(X, share, 1024)
+            own = pl.ds(pl.multiple_of(x * share, share), share)
+            xown[q, i] = part[q, i, core, own] + crecv[q, i, own]
         start(f"x{g}", q)
 
     def b2(q, g):
         arrived(f"x{g}", q)
         for i in range(*((0, 2), (2, 3))[g]):
-            xown[q, i] = (
-                xown[q, i] + xr[q, 0, i].astype(F32) + xr[q, 1, i].astype(F32) + xr[q, 2, i].astype(F32)
-            )
+            total = xown[q, i] + xr[q, 0, i].astype(F32) + xr[q, 1, i].astype(F32) + xr[q, 2, i].astype(F32)
+            xown[q, i] = total
+            zs[q, i] = total.astype(BF16)
         start(f"z{g}", q)
+
+    def summed(q, i):
+        return xown[q, i] + zr[q, i].astype(F32)
 
     def e_a(q):
         arrived("z0", q)
-        gate = xown[q, 0, zl] + zr[q, 0]
-        up = xown[q, 1, zl] + zr[q, 1]
-        zr[q, 0] = gate
-        zr[q, 1] = up
-        sigma = jax.nn.sigmoid(gate)
-        full[q, 0, core, x, zl] = (gate * sigma * up).astype(BF16)
-        start("back_z0", q)
+        gate, up = summed(q, 0), summed(q, 1)
+        full[q, 0, core, x] = (gate * jax.nn.sigmoid(gate) * up).astype(BF16)
+        start("back_x0", q)
 
     def e_b(q):
         arrived("z1", q)
-        gate = zr[q, 0]
-        up = zr[q, 1]
+        gate, up, grad = summed(q, 0), summed(q, 1), summed(q, 2)
         sigma = jax.nn.sigmoid(gate)
-        grad = xown[q, 2, zl] + zr[q, 2]
-        full[q, 1, core, x, zl] = (grad * up * sigma * (1.0 + gate * (1.0 - sigma))).astype(BF16)
-        full[q, 2, core, x, zl] = (grad * gate * sigma).astype(BF16)
-        start("back_z1", q)
+        full[q, 1, core, x] = (grad * up * sigma * (1.0 + gate * (1.0 - sigma))).astype(BF16)
+        full[q, 2, core, x] = (grad * gate * sigma).astype(BF16)
+        start("back_x1", q)
 
     def c1(q, g):
-        arrived(f"back_z{g}", q)
-        start(f"back_x{g}", q)
+        arrived(f"back_x{g}", q)
+        start(f"pass_x{g}", q)
 
     def c2(q, g):
-        arrived(f"back_x{g}", q)
+        arrived(f"pass_x{g}", q)
         start(f"back_c{g}", q)
 
     def g2a(q):
@@ -286,31 +287,29 @@
             gown[q, y] + gyr[q, 0].astype(F32) + gyr[q, 1].astype(F32) + gyr[q, 2].astype(F32)
         ).astype(BF16)
 
-    for copy in loads:
-        copy.start()
+    stages = dict(
+        a0=a0, a1t=a1t, a1c=a1c, g1a=g1a, g1b=g1b,
+        b1a=lambda q: b1(q, 0), b1b=lambda q: b1(q, 1),
+        b2a=lambda q: b2(q, 0), b2b=lambda q: b2(q, 1),
+        ea=e_a, eb=e_b,
+        c15a=lambda q: c1(q, 0), c15b=lambda q: c1(q, 1),
+        c2a=lambda q: c2(q, 0), c2b=lambda q: c2(q, 1),
+        g2a=g2a, g2b=g2b, d1a=d1a, d1b=d1b, d2a=d2a, d2b=d2b,
+    )
+
+    for i in range(3):
+        load(i).start()
     peers = [at_core, at_zl, at_zh] + [at_x(k) for k in (1, 2, 3)] + [at_y(k) for k in (1, 2, 3)]
     barrier = pltpu.get_barrier_semaphore()
     for peer in peers:
         pl.semaphore_signal(barrier, inc=1, device_id=peer, device_id_type=MESH)
     for q in range(CHUNKS):
-        for copy in own_copies(q):
-            copy.start()
+        own_copy(q, 0).start()
+        own_copy(q, 1).start()
     pl.semaphore_wait(barrier, len(peers))
-    a0(0)
-    for copy in loads:
-        copy.wait()
-
-    plan = PLAN(locals())
-    ticks = CHUNKS + max(delay for _, delay in plan)
-
-    @pl.loop(0, ticks)
-    def _(t):
-        for stage, delay in plan:
-            q = t - delay
-
-            @pl.when(jnp.logical_and(q >= 0, q < CHUNKS))
-            def _():
-                stage(q)
+
+    for stage, q in PLAN:
+        stages[stage](q)
 
     @pl.loop(0, CHUNKS)
     def _(q):
@@ -321,32 +320,25 @@
             out_copy(q, i).wait()
 
 
-def PLAN(s):
-    b1, b2, c1, c2 = s["b1"], s["b2"], s["c1"], s["c2"]
-
-    def next_a0(q):
-        @pl.when(q + 1 < CHUNKS)
-        def _():
-            s["a0"](q + 1)
-
-    return [
-        (s["e_a"], 2), (s["e_b"], 2),
-        (lambda q: b1(q, 0), 1), (lambda q: b1(q, 1), 1),
-        (s["g2a"], 3), (s["g2b"], 3),
-        (lambda q: c1(q, 0), 2), (lambda q: c1(q, 1), 2),
-        (s["a1"], 0), (next_a0, 0),
-        (lambda q: b2(q, 0), 1), (lambda q: b2(q, 1), 1),
-        (s["d1a"], 3), (s["d1b"], 3),
-        (s["g1a"], 0), (s["g1b"], 0),
-        (lambda q: c2(q, 0), 2), (lambda q: c2(q, 1), 2),
-        (s["d2a"], 3), (s["d2b"], 3),
-    ]
+PLAN = (
+    ("a0", 0), ("a1t", 0), ("a0", 2), ("a1c", 0), ("a1t", 2), ("g1a", 0), ("a0", 1), ("a1c", 2),
+    ("b1a", 0), ("g1b", 0), ("a0", 3), ("a1t", 1), ("b1b", 0), ("g1a", 2), ("g1b", 2), ("b2a", 0),
+    ("b1a", 2), ("b2b", 0), ("ea", 0), ("a1c", 1), ("eb", 0), ("b1b", 2), ("g1a", 1), ("a1t", 3),
+    ("a1c", 3), ("b1a", 1), ("b2a", 2), ("c15a", 0), ("g1b", 1), ("b2b", 2), ("c15b", 0), ("b1b", 1),
+    ("b2a", 1), ("g1a", 3), ("c2b", 0), ("ea", 2), ("c2a", 0), ("eb", 2), ("ea", 1), ("g2b", 0),
+    ("g1b", 3), ("c15a", 2), ("b1a", 3), ("c15b", 2), ("b1b", 3), ("g2a", 0), ("b2b", 1), ("c2a", 2),
+    ("g2a", 2), ("eb", 1), ("b2a", 3), ("c15a", 1), ("d1b", 0), ("c2b", 2), ("d1a", 0), ("ea", 3),
+    ("b2b", 3), ("g2b", 2), ("c15b", 1), ("c2a", 1), ("eb", 3), ("g2a", 1), ("c15a", 3), ("c2b", 1),
+    ("d1a", 2), ("c15b", 3), ("g2b", 1), ("d1b", 2), ("d2a", 0), ("c2a", 3), ("c2b", 3), ("g2a", 3),
+    ("g2b", 3), ("d2b", 0), ("d1b", 1), ("d1a", 3), ("d1a", 1), ("d1b", 3), ("d2a", 2), ("d2b", 2),
+    ("d2a", 1), ("d2a", 3), ("d2b", 1), ("d2b", 3),
+)
 
 
 def block(tokens, gate_weight, up_weight, down_weight, cotangent):
     n = CHUNKS
     rows, height = 128 // n, 1024 // n
-    share = height // 16
+    share = height // 8
     anyspace = pl.BlockSpec(memory_space=pl.ANY)
     vmem = pl.BlockSpec(memory_space=pltpu.VMEM)
     out_shape = [
@@ -354,18 +346,18 @@
         jax.ShapeDtypeStruct((128, 1152), BF16),
         jax.ShapeDtypeStruct((n, Y, 2, rows, 1152), BF16),
         jax.ShapeDtypeStruct((n, Y, 2, rows, 1152), BF16),
-        jax.ShapeDtypeStruct((n, 2, X, 2, share, 1024), BF16),
-        jax.ShapeDtypeStruct((n, 2, X, 2, share, 1024), BF16),
-        jax.ShapeDtypeStruct((n, 2, X, 2, share, 1024), BF16),
+        jax.ShapeDtypeStruct((n, 2, X, share, 1024), BF16),
+        jax.ShapeDtypeStruct((n, 2, X, share, 1024), BF16),
+        jax.ShapeDtypeStruct((n, 2, X, share, 1024), BF16),
     ]
     V = pltpu.VMEM
     scratch = [
         V((1152, 1024), BF16), V((1152, 1024), BF16), V((1024, 1152), BF16),
         V((n, Y, 2, rows, 1152), BF16), V((n, Y, 2, rows, 1152), BF16),
-        V((2, 3, 2, height // 2, 1024), F32), V((n, 3, height // 2, 1024), F32),
-        V((n, 3, X, 2, share, 1024), BF16), V((n, 3, 3, 2, share, 1024), BF16),
-        V((n, 3, 2, share, 1024), F32), V((n, 3, share, 1024), F32),
-        V((n, 3, 2, X, 2, share, 1024), BF16),
+        V((n, 3, 2, height // 2, 1024), F32), V((n, 3, height // 2, 1024), F32),
+        V((n, 3, X, share, 1024), BF16), V((n, 3, 3, share, 1024), BF16),
+        V((n, 3, share, 1024), F32), V((n, 3, share, 1024), BF16), V((n, 3, share, 1024), BF16),
+        V((n, 3, 2, X, share, 1024), BF16),
         V((Y, 2, rows, 1152), F32),
         V((n, Y, 2, rows, 1152), BF16), V((n, 2, rows, 1152), F32), V((n, 3, 2, rows, 1152), BF16),
         V((n, rows, 1152), BF16), V((n, rows, 1152), BF16),
@@ -381,11 +373,73 @@
         out_specs=[vmem, vmem] + [anyspace] * 5,
         scratch_shapes=scratch,
         compiler_params=pltpu.CompilerParams(
-            collective_id=0, has_side_effects=True, vmem_limit_bytes=62 << 20
+            collective_id=0, has_side_effects=True, vmem_limit_bytes=63 << 20
         ),
         cost_estimate=pl.CostEstimate(flops=14_500_000_000, bytes_accessed=30_000_000, transcendentals=0),
         name="exchange",
     )(tokens, gate_weight, up_weight, down_weight, cotangent)
+
+
+def gradients_kernel(
+    tok, cot, hid, ggp, gup, grad_gate, grad_up, grad_down,
+    tok_v, cot_v, hid_v, ggp_v, gup_v, gate_v, up_v, down_v, in_sem, out_sem,
+):
+    pairs = ((tok, tok_v), (ggp, ggp_v), (gup, gup_v), (hid, hid_v), (cot, cot_v))
+    loads = [pltpu.make_async_copy(src, dst, in_sem.at[i]) for i, (src, dst) in enumerate(pairs)]
+    loads[0].start()
+    loads[1].start()
+
+    def product(left, right, total, out, height, group):
+        def write(m):
+            part = pl.ds(pl.multiple_of(m * height, height), height)
+            return pltpu.make_async_copy(total.at[part], out.at[part], out_sem.at[group, m])
+
+        tiles = left.shape[1] // height
+
+        @pl.loop(0, tiles)
+        def _(m):
+            part = pl.ds(pl.multiple_of(m * height, height), height)
+            total[part, :] = inner_rows(left[:, part], right[...])
+            write(m).start()
+
+        return [write(m) for m in range(tiles)]
+
+    loads[0].wait()
+    loads[1].wait()
+    for copy in loads[2:]:
+        copy.start()
+    writes = product(tok_v, ggp_v, gate_v, grad_gate, TILE_A, 0)
+    loads[2].wait()
+    writes += product(tok_v, gup_v, up_v, grad_up, TILE_A, 1)
+    loads[3].wait()
+    loads[4].wait()
+    writes += product(hid_v, cot_v, down_v, grad_down, TILE_B, 2)
+    for copy in writes:
+        copy.wait()
+
+
+TILE_A, TILE_B = 384, 256
+
+
+def weight_gradients(rows_all, cot_all, hidden, ggp, gup):
+    wide, tall = (1024, 1152), (1152, 1024)
+    square = (1024, 1024)
+    V = pltpu.VMEM
+    anyspace = pl.BlockSpec(memory_space=pl.ANY)
+    return pl.pallas_call(
+        gradients_kernel,
+        out_shape=[jax.ShapeDtypeStruct(s, F32) for s in (tall, tall, wide)],
+        in_specs=[anyspace] * 5,
+        out_specs=[anyspace] * 3,
+        scratch_shapes=[
+            V(wide, BF16), V(wide, BF16), V(square, BF16), V(square, BF16), V(square, BF16),
+            V(tall, F32), V(tall, F32), V(wide, F32),
+            pltpu.SemaphoreType.DMA((5,)), pltpu.SemaphoreType.DMA((3, 8)),
+        ],
+        compiler_params=pltpu.CompilerParams(vmem_limit_bytes=63 << 20),
+        cost_estimate=pl.CostEstimate(flops=7_250_000_000, bytes_accessed=25_000_000, transcendentals=0),
+        name="weight_gradients",
+    )(rows_all, cot_all, hidden, ggp, gup)
 
 
 def on_device(tokens, gate_weight, up_weight, down_weight, cotangent):
@@ -395,9 +449,7 @@
     rows_all = rows_all.reshape(1024, 1152)
     cot_all = cot_all.reshape(1024, 1152)
     hidden, ggp, gup = (a.reshape(1024, 1024) for a in (hidden, ggp, gup))
-    grad_gate = inner_rows(rows_all, ggp)
-    grad_up = inner_rows(rows_all, gup)
-    grad_down = inner_rows(hidden, cot_all)
+    grad_gate, grad_up, grad_down = weight_gradients(rows_all, cot_all, hidden, ggp, gup)
     return (mixed, grad_tokens, grad_gate, grad_up, grad_down)
 
 

time: 164 us -> 131 us (0.80)
  matrix products: 16.2 us -> 0 us
  Pallas kernels: 145 us -> 129 us
    pallas_call x1, Pallas kernels: 145 us -> 115 us  [block(): pl.pallas_call(kernel, out_shape=out_shape, in_specs=[anyspace] * 5, out_...]
    dot_general x3 -> x0, matrix products: 16.2 us -> none  [inner_rows(): lax.dot_general(left, right, (((0,), (0,)), ((), ())), preferred_element_...]
    pallas_call x0 -> x1, Pallas kernels: none -> 13.3 us  [weight_gradients(): pl.pallas_call(gradients_kernel, out_shape=[jax.ShapeDtypeStruct(s, F32)...]
where the time goes in v3:
time: 131 us
  Pallas kernels  129 us (98%)
  local copies, waits for them, and re-layouts  1.44 us (1%)
    pallas_call x1, Pallas kernels, block(): pl.pallas_call(kernel, out_shape=out_shape, in_specs=[anyspace] * 5, out_...  115 us
    pallas_call x1, Pallas kernels, weight_gradients(): pl.pallas_call(gradients_kernel, out_shape=[jax.ShapeDtypeStruct(s, F32)...  13.3 us

profile of v3, /device:TPU:0, one launch (start us, length us, event | category | flops | bytes accessed | tf_op | source)
XLA Modules:
  0.0 130.6 jit_solution(760728485207071711)
XLA Ops:
  0.6 115.2 %exchange.1 = (bf16[128,1152]{1,0:T(8,128)(2,1)}, bf16[128,1152]{1,0:T(8,128)(2,1)}, bf16[4,4,2,32,1152]{4,3,2,1,0:T(8,128)(2,1)}, bf16[4,4,2,32,1152]{4,3,2,1,0...) custom-call(bf16[128,1152]{1,0:T(8,128)(2,1)} %tokens.1, ...), custom_call_target="tpu_custom_call" | custom-call | flops 14499999744 | bytes 30000000 | tf_op jit(solution)/shard_map/exchange/pallas_call | solution.py:369
  115.9 0.0 copy-start.1
  115.9 0.0 copy-start
  115.9 13.3 %weight_gradients.1 = (f32[1152,1024]{1,0:T(8,128)}, f32[1152,1024]{1,0:T(8,128)}, f32[1024,1152]{1,0:T(8,128)}) custom-call(bf16[1024,1152]{1,0:T(8,128)(2,1)} %bitcast.5, bf16[1024,1152]{1,0:T(8,128)(2,1)} %bitcast.6, bf16[1024,1024]{1,0:T(8,128)(2,1)} %bitcast.7, bf16[1024,1024]{1,0:T(8,128)(2,1)} %bitcast.8, bf16[1024,1024]{1,0:T(8,128)(2,1)} %bitcast.9), custom_call_target="tpu_custom_call" | custom-call | flops 7249999872 | bytes 25000000 | tf_op jit(solution)/shard_map/weight_gradients/pallas_call | solution.py:429
  129.2 0.0 copy-done.1
  129.2 0.7 copy.12
  129.9 0.0 copy-done
  129.9 0.7 copy.13
Async XLA Ops:
  115.9 13.3 %copy-start.1 = (bf16[128,1152]{1,0:T(8,128)(2,1)S(1)}, bf16[128,1152]{1,0:T(8,128)(2,1)}, u32[]{:S(2)}) copy-start(bf16[128,1152]{1,0:T(8,128)(2,1)} %get-tuple-element.30) | copy-start | bytes 884740
  115.9 14.0 %copy-start = (bf16[128,1152]{1,0:T(8,128)(2,1)S(1)}, bf16[128,1152]{1,0:T(8,128)(2,1)}, u32[]{:S(2)}) copy-start(bf16[128,1152]{1,0:T(8,128)(2,1)} %get-tuple-element.31) | copy-start | bytes 884740

commit v4 on v3

--- a/solution.py
+++ b/solution.py
@@ -40,7 +40,7 @@
 def kernel(
     tokens, gate_w, up_w, down_w, cotangent,
     mixed, grad_tokens, tok_out, cot_out, hid_out, ggp_out, gup_out,
-    gw, uw, dw, tok, cot, part, crecv, xs, xr, xown, zs, zr, full, tmp,
+    gw, uw, dw, tok, cot, part, crecv, xs, xr, xown, zr, full, tmp, tok_t, hid_t,
     ms, mown, mr, mz, mzr, gs, gown, gr, gys, gyr,
     send_sem, recv_sem, load_sem, own_sem, out_sem,
 ):
@@ -88,17 +88,17 @@
         if name == "tok_z":
             return [remote(name, q, 0, tokens.at[mine(q)], tok.at[q, y, zh], at_zh)]
         if name == "cot_y":
-            return [remote(name, q, k - 1, cotangent.at[mine(q)], cot.at[q, y, zh], at_y(k)) for k in (1, 3, 2)]
+            return [remote(name, q, k - 1, cotangent.at[mine(q)], cot.at[q, y, zh], at_y(k)) for k in (2, 1, 3)]
         if name == "tok_y":
-            return [remote(name, q, k - 1, tok.at[q, y], tok.at[q, y], at_y(k)) for k in (1, 3, 2)]
+            return [remote(name, q, k - 1, tok.at[q, y], tok.at[q, y], at_y(k)) for k in (2, 1, 3)]
         if name == "cot_z":
             return [remote(name, q, 0, cot.at[q, :, zh], cot.at[q, :, zh], at_zh)]
         if kind == "core":
             return [remote(name, q, 0, part.at[q, GROUP[g], 1 - core], crecv.at[q, GROUP[g]], at_core)]
         if kind == "x":
-            return [remote(name, q, k - 1, xs.at[q, GROUP[g], lax.rem(x + k, 4)], xr.at[q, k - 1, GROUP[g]], at_x(k)) for k in (1, 3, 2)]
+            return [remote(name, q, k - 1, xs.at[q, GROUP[g], lax.rem(x + k, 4)], xr.at[q, k - 1, GROUP[g]], at_x(k)) for k in (2, 1, 3)]
         if kind == "z":
-            return [remote(name, q, 0, zs.at[q, GROUP[g]], zr.at[q, GROUP[g]], at_zl)]
+            return [remote(name, q, 0, xs.at[q, GROUP[g], x], zr.at[q, GROUP[g]], at_zl)]
         if kind == "back_x":
             ref = full.at[q, BACK[g], core, x]
             return [remote(name, q, i, ref, ref, at_x(k)) for i, k in enumerate((1, 3))]
@@ -112,13 +112,13 @@
             ref = full.at[q, BACK[g], core]
             return [remote(name, q, 0, ref, ref, at_core)]
         if name == "mix_y":
-            return [remote(name, q, k - 1, ms.at[q, lax.rem(y + k, 4)], mr.at[q, k - 1], at_y(k)) for k in (1, 3, 2)]
+            return [remote(name, q, k - 1, ms.at[q, lax.rem(y + k, 4)], mr.at[q, k - 1], at_y(k)) for k in (2, 1, 3)]
         if name == "mix_z":
             return [remote(name, q, 0, mz.at[q], mzr.at[q], at_zh)]
         if name == "gt_z":
             return [remote(name, q, 0, gs.at[q, :, 1 - zh], gr.at[q], at_zh)]
         if name == "gt_y":
-            return [remote(name, q, k - 1, gys.at[q, lax.rem(y + k, 4)], gyr.at[q, k - 1], at_y(k)) for k in (1, 3, 2)]
+            return [remote(name, q, k - 1, gys.at[q, lax.rem(y + k, 4)], gyr.at[q, k - 1], at_y(k)) for k in (2, 1, 3)]
 
     def start(name, q):
         for copy in copies(name, q):
@@ -141,8 +141,9 @@
         return pltpu.make_async_copy(src, dst, load_sem.at[i])
 
     def out_copy(q, i):
-        src = (tok.at[q], cot.at[q], full.at[q, 0], full.at[q, 1], full.at[q, 2])[i]
-        dst = (tok_out, cot_out, hid_out, ggp_out, gup_out)[i].at[q]
+        part = pl.ds(q * height, height)
+        src = (tok_t.at[:, part], cot.at[q], hid_t.at[:, part], full.at[q, 1], full.at[q, 2])[i]
+        dst = (tok_out.at[:, part], cot_out.at[q], hid_out.at[:, part], ggp_out.at[q], gup_out.at[q])[i]
         return pltpu.make_async_copy(src, dst, out_sem.at[q, i])
 
     def a0(q):
@@ -161,10 +162,9 @@
 
     def g1a(q):
         arrived("tok_y", q)
-        if q == 0:
+        if q == next(c for stage, c in PLAN if stage == "g1a"):
             load(0).wait()
             load(1).wait()
-        out_copy(q, 0).start()
         block = tok[q].reshape(height, 1152)
         slot = q
 
@@ -175,10 +175,12 @@
             part[slot, 1, :, :, cols] = dot(block, uw[:, cols]).reshape(2, height // 2, 256)
 
         start("core0", q)
+        tok_t[:, pl.ds(q * height, height)] = block.T
+        out_copy(q, 0).start()
 
     def g1b(q):
         arrived("cot_z", q)
-        if q == 0:
+        if q == next(c for stage, c in PLAN if stage == "g1b"):
             load(2).wait()
         out_copy(q, 1).start()
         block = cot[q].reshape(height, 1152)
@@ -206,7 +208,7 @@
         for i in range(*((0, 2), (2, 3))[g]):
             total = xown[q, i] + xr[q, 0, i].astype(F32) + xr[q, 1, i].astype(F32) + xr[q, 2, i].astype(F32)
             xown[q, i] = total
-            zs[q, i] = total.astype(BF16)
+            xs[q, i, x] = total.astype(BF16)
         start(f"z{g}", q)
 
     def summed(q, i):
@@ -236,7 +238,6 @@
 
     def g2a(q):
         arrived("back_c0", q)
-        out_copy(q, 2).start()
         block = full[q, 0].reshape(height, 1024)
 
         @pl.loop(0, 3)
@@ -247,6 +248,8 @@
         ms[q] = tmp[...].astype(BF16)
         mown[q] = tmp[y]
         start("mix_y", q)
+        hid_t[:, pl.ds(q * height, height)] = block.T
+        out_copy(q, 2).start()
 
     def g2b(q):
         arrived("back_c1", q)
@@ -297,8 +300,6 @@
         g2a=g2a, g2b=g2b, d1a=d1a, d1b=d1b, d2a=d2a, d2b=d2b,
     )
 
-    for i in range(3):
-        load(i).start()
     peers = [at_core, at_zl, at_zh] + [at_x(k) for k in (1, 2, 3)] + [at_y(k) for k in (1, 2, 3)]
     barrier = pltpu.get_barrier_semaphore()
     for peer in peers:
@@ -308,30 +309,35 @@
         own_copy(q, 1).start()
     pl.semaphore_wait(barrier, len(peers))
 
-    for stage, q in PLAN:
+    for step, (stage, q) in enumerate(PLAN):
         stages[stage](q)
+        if step == 0:
+            for i in range(3):
+                load(i).start()
 
     @pl.loop(0, CHUNKS)
     def _(q):
         for name in COLUMNS:
             if not name.startswith("core"):
                 sent(name, q)
+
+    for q in range(CHUNKS):
         for i in range(5):
             out_copy(q, i).wait()
 
 
 PLAN = (
-    ("a0", 0), ("a1t", 0), ("a0", 2), ("a1c", 0), ("a1t", 2), ("g1a", 0), ("a0", 1), ("a1c", 2),
-    ("b1a", 0), ("g1b", 0), ("a0", 3), ("a1t", 1), ("b1b", 0), ("g1a", 2), ("g1b", 2), ("b2a", 0),
-    ("b1a", 2), ("b2b", 0), ("ea", 0), ("a1c", 1), ("eb", 0), ("b1b", 2), ("g1a", 1), ("a1t", 3),
-    ("a1c", 3), ("b1a", 1), ("b2a", 2), ("c15a", 0), ("g1b", 1), ("b2b", 2), ("c15b", 0), ("b1b", 1),
-    ("b2a", 1), ("g1a", 3), ("c2b", 0), ("ea", 2), ("c2a", 0), ("eb", 2), ("ea", 1), ("g2b", 0),
-    ("g1b", 3), ("c15a", 2), ("b1a", 3), ("c15b", 2), ("b1b", 3), ("g2a", 0), ("b2b", 1), ("c2a", 2),
-    ("g2a", 2), ("eb", 1), ("b2a", 3), ("c15a", 1), ("d1b", 0), ("c2b", 2), ("d1a", 0), ("ea", 3),
-    ("b2b", 3), ("g2b", 2), ("c15b", 1), ("c2a", 1), ("eb", 3), ("g2a", 1), ("c15a", 3), ("c2b", 1),
-    ("d1a", 2), ("c15b", 3), ("g2b", 1), ("d1b", 2), ("d2a", 0), ("c2a", 3), ("c2b", 3), ("g2a", 3),
-    ("g2b", 3), ("d2b", 0), ("d1b", 1), ("d1a", 3), ("d1a", 1), ("d1b", 3), ("d2a", 2), ("d2b", 2),
-    ("d2a", 1), ("d2a", 3), ("d2b", 1), ("d2b", 3),
+    ("a0", 0), ("a0", 2), ("a1c", 0), ("a1t", 0), ("a1t", 2), ("a1c", 2), ("g1b", 0), ("g1a", 0),
+    ("b1b", 0), ("b1a", 0), ("a0", 3), ("g1b", 2), ("b2b", 0), ("a0", 1), ("g1a", 2), ("a1t", 3),
+    ("b1b", 2), ("b1a", 2), ("b2a", 0), ("a1c", 3), ("ea", 0), ("eb", 0), ("a1t", 1), ("g1a", 3),
+    ("b2b", 2), ("b2a", 2), ("c15a", 0), ("b1a", 3), ("ea", 2), ("c15b", 0), ("c2a", 0), ("a1c", 1),
+    ("g1b", 3), ("eb", 2), ("g1a", 1), ("b1b", 3), ("c2b", 0), ("b2a", 3), ("c15a", 2), ("g2a", 0),
+    ("b1a", 1), ("c15b", 2), ("g2b", 0), ("g1b", 1), ("b2b", 3), ("c2a", 2), ("b1b", 1), ("ea", 3),
+    ("g2a", 2), ("b2a", 1), ("eb", 3), ("c2b", 2), ("b2b", 1), ("c15a", 3), ("ea", 1), ("g2b", 2),
+    ("c15b", 3), ("d1b", 0), ("d1a", 2), ("c2a", 3), ("eb", 1), ("g2a", 3), ("c15a", 1), ("c2b", 3),
+    ("c15b", 1), ("g2b", 3), ("c2a", 1), ("d1b", 2), ("d2b", 0), ("c2b", 1), ("g2a", 1), ("g2b", 1),
+    ("d2a", 2), ("d1b", 3), ("d1a", 0), ("d2b", 2), ("d1a", 3), ("d1b", 1), ("d1a", 1), ("d2a", 3),
+    ("d2b", 3), ("d2a", 1), ("d2a", 0), ("d2b", 1),
 )
 
 
@@ -344,9 +350,9 @@
     out_shape = [
         jax.ShapeDtypeStruct((128, 1152), BF16),
         jax.ShapeDtypeStruct((128, 1152), BF16),
+        jax.ShapeDtypeStruct((1152, 1024), BF16),
         jax.ShapeDtypeStruct((n, Y, 2, rows, 1152), BF16),
-        jax.ShapeDtypeStruct((n, Y, 2, rows, 1152), BF16),
-        jax.ShapeDtypeStruct((n, 2, X, share, 1024), BF16),
+        jax.ShapeDtypeStruct((1024, 1024), BF16),
         jax.ShapeDtypeStruct((n, 2, X, share, 1024), BF16),
         jax.ShapeDtypeStruct((n, 2, X, share, 1024), BF16),
     ]
@@ -356,9 +362,9 @@
         V((n, Y, 2, rows, 1152), BF16), V((n, Y, 2, rows, 1152), BF16),
         V((n, 3, 2, height // 2, 1024), F32), V((n, 3, height // 2, 1024), F32),
         V((n, 3, X, share, 1024), BF16), V((n, 3, 3, share, 1024), BF16),
-        V((n, 3, share, 1024), F32), V((n, 3, share, 1024), BF16), V((n, 3, share, 1024), BF16),
+        V((n, 3, share, 1024), F32), V((n, 3, share, 1024), BF16),
         V((n, 3, 2, X, share, 1024), BF16),
-        V((Y, 2, rows, 1152), F32),
+        V((Y, 2, rows, 1152), F32), V((1152, 1024), BF16), V((1024, 1024), BF16),
         V((n, Y, 2, rows, 1152), BF16), V((n, 2, rows, 1152), F32), V((n, 3, 2, rows, 1152), BF16),
         V((n, rows, 1152), BF16), V((n, rows, 1152), BF16),
         V((n, Y, 2, rows, 1152), BF16), V((n, Y, rows, 1152), F32), V((n, Y, rows, 1152), BF16),
@@ -381,75 +387,90 @@
 
 
 def gradients_kernel(
-    tok, cot, hid, ggp, gup, grad_gate, grad_up, grad_down,
-    tok_v, cot_v, hid_v, ggp_v, gup_v, gate_v, up_v, down_v, in_sem, out_sem,
+    tok, cot, hid, ggp, gup, mixed_in, tokens_in,
+    grad_gate, grad_up, grad_down, mixed, grad_tokens,
+    tok_v, cot_v, hid_v, ggp_v, gup_v, gate_v, up_v, down_v, small_v, in_sem, out_sem, pass_sem,
 ):
     pairs = ((tok, tok_v), (ggp, ggp_v), (gup, gup_v), (hid, hid_v), (cot, cot_v))
     loads = [pltpu.make_async_copy(src, dst, in_sem.at[i]) for i, (src, dst) in enumerate(pairs)]
+    taken = [
+        pltpu.make_async_copy(mixed_in, small_v.at[0], pass_sem.at[0]),
+        pltpu.make_async_copy(tokens_in, small_v.at[1], pass_sem.at[1]),
+    ]
+    handed = [
+        pltpu.make_async_copy(small_v.at[0], mixed, pass_sem.at[2]),
+        pltpu.make_async_copy(small_v.at[1], grad_tokens, pass_sem.at[3]),
+    ]
     loads[0].start()
     loads[1].start()
 
     def product(left, right, total, out, height, group):
-        def write(m):
-            part = pl.ds(pl.multiple_of(m * height, height), height)
-            return pltpu.make_async_copy(total.at[part], out.at[part], out_sem.at[group, m])
-
-        tiles = left.shape[1] // height
+        def write(n):
+            part = pl.ds(pl.multiple_of(n * height, height), height)
+            return pltpu.make_async_copy(total.at[part], out.at[part], out_sem.at[group, n])
+
+        tiles = left.shape[0] // height
 
         @pl.loop(0, tiles)
-        def _(m):
-            part = pl.ds(pl.multiple_of(m * height, height), height)
-            total[part, :] = inner_rows(left[:, part], right[...])
-            write(m).start()
-
-        return [write(m) for m in range(tiles)]
+        def _(n):
+            part = pl.ds(pl.multiple_of(n * height, height), height)
+            total[part, :] = dot(left[part, :], right[...])
+            write(n).start()
+
+        return [write(n) for n in range(tiles)]
 
     loads[0].wait()
     loads[1].wait()
-    for copy in loads[2:]:
+    for copy in loads[2:] + taken:
         copy.start()
     writes = product(tok_v, ggp_v, gate_v, grad_gate, TILE_A, 0)
+    for copy in taken:
+        copy.wait()
+    for copy in handed:
+        copy.start()
     loads[2].wait()
     writes += product(tok_v, gup_v, up_v, grad_up, TILE_A, 1)
     loads[3].wait()
     loads[4].wait()
     writes += product(hid_v, cot_v, down_v, grad_down, TILE_B, 2)
-    for copy in writes:
+    for copy in writes + handed:
         copy.wait()
 
 
-TILE_A, TILE_B = 384, 256
-
-
-def weight_gradients(rows_all, cot_all, hidden, ggp, gup):
+TILE_A, TILE_B = 576, 512
+
+
+def weight_gradients(rows_all, cot_all, hidden, ggp, gup, mixed, grad_tokens):
     wide, tall = (1024, 1152), (1152, 1024)
-    square = (1024, 1024)
+    square, small = (1024, 1024), (128, 1152)
     V = pltpu.VMEM
     anyspace = pl.BlockSpec(memory_space=pl.ANY)
+    shapes = [jax.ShapeDtypeStruct(s, F32) for s in (tall, tall, wide)]
     return pl.pallas_call(
         gradients_kernel,
-        out_shape=[jax.ShapeDtypeStruct(s, F32) for s in (tall, tall, wide)],
-        in_specs=[anyspace] * 5,
-        out_specs=[anyspace] * 3,
+        out_shape=shapes + [jax.ShapeDtypeStruct(small, BF16)] * 2,
+        in_specs=[anyspace] * 7,
+        out_specs=[anyspace] * 5,
         scratch_shapes=[
-            V(wide, BF16), V(wide, BF16), V(square, BF16), V(square, BF16), V(square, BF16),
-            V(tall, F32), V(tall, F32), V(wide, F32),
-            pltpu.SemaphoreType.DMA((5,)), pltpu.SemaphoreType.DMA((3, 8)),
+            V(tall, BF16), V(wide, BF16), V(square, BF16), V(square, BF16), V(square, BF16),
+            V(tall, F32), V(tall, F32), V(wide, F32), V((2,) + small, BF16),
+            pltpu.SemaphoreType.DMA((5,)), pltpu.SemaphoreType.DMA((3, 8)), pltpu.SemaphoreType.DMA((4,)),
         ],
         compiler_params=pltpu.CompilerParams(vmem_limit_bytes=63 << 20),
         cost_estimate=pl.CostEstimate(flops=7_250_000_000, bytes_accessed=25_000_000, transcendentals=0),
         name="weight_gradients",
-    )(rows_all, cot_all, hidden, ggp, gup)
+    )(rows_all, cot_all, hidden, ggp, gup, mixed, grad_tokens)
 
 
 def on_device(tokens, gate_weight, up_weight, down_weight, cotangent):
     mixed, grad_tokens, rows_all, cot_all, hidden, ggp, gup = block(
         tokens, gate_weight, up_weight, down_weight, cotangent
     )
-    rows_all = rows_all.reshape(1024, 1152)
     cot_all = cot_all.reshape(1024, 1152)
-    hidden, ggp, gup = (a.reshape(1024, 1024) for a in (hidden, ggp, gup))
-    grad_gate, grad_up, grad_down = weight_gradients(rows_all, cot_all, hidden, ggp, gup)
+    ggp, gup = ggp.reshape(1024, 1024), gup.reshape(1024, 1024)
+    grad_gate, grad_up, grad_down, mixed, grad_tokens = weight_gradients(
+        rows_all, cot_all, hidden, ggp, gup, mixed, grad_tokens
+    )
     return (mixed, grad_tokens, grad_gate, grad_up, grad_down)
 
 

time: 131 us -> 130 us (level)
  local copies, waits for them, and re-layouts: 1.44 us -> 0 us
    unnamed x6 -> x0, local copies, waits for them, and re-layouts: 1.44 us -> none
where the time goes in v4:
time: 130 us
  Pallas kernels  129 us (99%)
    pallas_call x1, Pallas kernels, block(): pl.pallas_call(kernel, out_shape=out_shape, in_specs=[anyspace] * 5, out_...  115 us
    pallas_call x1, Pallas kernels, weight_gradients(): pl.pallas_call(gradients_kernel, out_shape=shapes + [jax.ShapeDtypeStruct...  14.1 us

profile of v4, /device:TPU:0, one launch (start us, length us, event | category | flops | bytes accessed | tf_op | source)
XLA Modules:
  0.0 129.6 jit_solution(5940102764308715187)
XLA Ops:
  0.6 114.7 %exchange.1 = (bf16[128,1152]{1,0:T(8,128)(2,1)}, bf16[128,1152]{1,0:T(8,128)(2,1)}, bf16[1152,1024]{1,0:T(8,128)(2,1)}, bf16[4,4,2,32,1152]{4,3,2,1,0:T(8,128)(...) custom-call(bf16[128,1152]{1,0:T(8,128)(2,1)} %tokens.1, ...), custom_call_target="tpu_custom_call" | custom-call | flops 14499999744 | bytes 30000000 | tf_op jit(solution)/shard_map/exchange/pallas_call | solution.py:375
  115.3 14.1 %weight_gradients.1 = (f32[1152,1024]{1,0:T(8,128)}, f32[1152,1024]{1,0:T(8,128)}, f32[1024,1152]{1,0:T(8,128)}, bf16[128,1152]{1,0:T(8,128)(2,1)}, bf16[128,1152]{1,0:T(8,128)(2,1)}) custom-call(bf16[1152,1024]{1,0:T(8,128)(2,1)} %get-tuple-element.17.tok, bf16[1024,1152]{1,0:T(8,128)(2,1)} %bitcast.3, bf16[1024,1024]{1,0:T(8,128)(2,1)} %get-tuple-element.19.hid, ...), custom_call_target="tpu_custom_call" | custom-call | flops 7249999872 | bytes 25000000 | tf_op jit(solution)/shard_map/weight_gradients/pallas_call | solution.py:449

commit v5 on v3

--- a/solution.py
+++ b/solution.py
@@ -88,15 +88,15 @@
         if name == "tok_z":
             return [remote(name, q, 0, tokens.at[mine(q)], tok.at[q, y, zh], at_zh)]
         if name == "cot_y":
-            return [remote(name, q, k - 1, cotangent.at[mine(q)], cot.at[q, y, zh], at_y(k)) for k in (1, 3, 2)]
+            return [remote(name, q, k - 1, cotangent.at[mine(q)], cot.at[q, y, zh], at_y(k)) for k in (2, 1, 3)]
         if name == "tok_y":
-            return [remote(name, q, k - 1, tok.at[q, y], tok.at[q, y], at_y(k)) for k in (1, 3, 2)]
+            return [remote(name, q, k - 1, tok.at[q, y], tok.at[q, y], at_y(k)) for k in (2, 1, 3)]
         if name == "cot_z":
             return [remote(name, q, 0, cot.at[q, :, zh], cot.at[q, :, zh], at_zh)]
         if kind == "core":
             return [remote(name, q, 0, part.at[q, GROUP[g], 1 - core], crecv.at[q, GROUP[g]], at_core)]
         if kind == "x":
-            return [remote(name, q, k - 1, xs.at[q, GROUP[g], lax.rem(x + k, 4)], xr.at[q, k - 1, GROUP[g]], at_x(k)) for k in (1, 3, 2)]
+            return [remote(name, q, k - 1, xs.at[q, GROUP[g], lax.rem(x + k, 4)], xr.at[q, k - 1, GROUP[g]], at_x(k)) for k in (2, 1, 3)]
         if kind == "z":
             return [remote(name, q, 0, zs.at[q, GROUP[g]], zr.at[q, GROUP[g]], at_zl)]
         if kind == "back_x":
@@ -112,13 +112,13 @@
             ref = full.at[q, BACK[g], core]
             return [remote(name, q, 0, ref, ref, at_core)]
         if name == "mix_y":
-            return [remote(name, q, k - 1, ms.at[q, lax.rem(y + k, 4)], mr.at[q, k - 1], at_y(k)) for k in (1, 3, 2)]
+            return [remote(name, q, k - 1, ms.at[q, lax.rem(y + k, 4)], mr.at[q, k - 1], at_y(k)) for k in (2, 1, 3)]
         if name == "mix_z":
             return [remote(name, q, 0, mz.at[q], mzr.at[q], at_zh)]
         if name == "gt_z":
             return [remote(name, q, 0, gs.at[q, :, 1 - zh], gr.at[q], at_zh)]
         if name == "gt_y":
-            return [remote(name, q, k - 1, gys.at[q, lax.rem(y + k, 4)], gyr.at[q, k - 1], at_y(k)) for k in (1, 3, 2)]
+            return [remote(name, q, k - 1, gys.at[q, lax.rem(y + k, 4)], gyr.at[q, k - 1], at_y(k)) for k in (2, 1, 3)]
 
     def start(name, q):
         for copy in copies(name, q):
@@ -297,8 +297,6 @@
         g2a=g2a, g2b=g2b, d1a=d1a, d1b=d1b, d2a=d2a, d2b=d2b,
     )
 
-    for i in range(3):
-        load(i).start()
     peers = [at_core, at_zl, at_zh] + [at_x(k) for k in (1, 2, 3)] + [at_y(k) for k in (1, 2, 3)]
     barrier = pltpu.get_barrier_semaphore()
     for peer in peers:
@@ -308,8 +306,11 @@
         own_copy(q, 1).start()
     pl.semaphore_wait(barrier, len(peers))
 
-    for stage, q in PLAN:
+    for step, (stage, q) in enumerate(PLAN):
         stages[stage](q)
+        if step == 0:
+            for i in range(3):
+                load(i).start()
 
     @pl.loop(0, CHUNKS)
     def _(q):

time: 131 us -> 130 us (level)
  no operation moved by 1% of the time
where the time goes in v5:
time: 130 us
  Pallas kernels  128 us (98%)
  local copies, waits for them, and re-layouts  1.44 us (1%)
    pallas_call x1, Pallas kernels, block(): pl.pallas_call(kernel, out_shape=out_shape, in_specs=[anyspace] * 5, out_...  115 us
    pallas_call x1, Pallas kernels, weight_gradients(): pl.pallas_call(gradients_kernel, out_shape=[jax.ShapeDtypeStruct(s, F32)...  13.3 us

profile of v5, /device:TPU:0, one launch (start us, length us, event | category | flops | bytes accessed | tf_op | source)
XLA Modules:
  0.0 129.9 jit_solution(17300299198689970677)
XLA Ops:
  0.6 114.5 %exchange.1 = (bf16[128,1152]{1,0:T(8,128)(2,1)}, bf16[128,1152]{1,0:T(8,128)(2,1)}, bf16[4,4,2,32,1152]{4,3,2,1,0:T(8,128)(2,1)}, bf16[4,4,2,32,1152]{4,3,2,1,0...) custom-call(bf16[128,1152]{1,0:T(8,128)(2,1)} %tokens.1, ...), custom_call_target="tpu_custom_call" | custom-call | flops 14499999744 | bytes 30000000 | tf_op jit(solution)/shard_map/exchange/pallas_call | solution.py:370
  115.2 0.0 copy-start.1
  115.2 0.0 copy-start
  115.2 13.3 %weight_gradients.1 = (f32[1152,1024]{1,0:T(8,128)}, f32[1152,1024]{1,0:T(8,128)}, f32[1024,1152]{1,0:T(8,128)}) custom-call(bf16[1024,1152]{1,0:T(8,128)(2,1)} %bitcast.5, bf16[1024,1152]{1,0:T(8,128)(2,1)} %bitcast.6, bf16[1024,1024]{1,0:T(8,128)(2,1)} %bitcast.7, bf16[1024,1024]{1,0:T(8,128)(2,1)} %bitcast.8, bf16[1024,1024]{1,0:T(8,128)(2,1)} %bitcast.9), custom_call_target="tpu_custom_call" | custom-call | flops 7249999872 | bytes 25000000 | tf_op jit(solution)/shard_map/weight_gradients/pallas_call | solution.py:430
  128.5 0.0 copy-done.1
  128.5 0.7 copy.12
  129.2 0.0 copy-done
  129.2 0.7 copy.13
Async XLA Ops:
  115.2 13.3 %copy-start.1 = (bf16[128,1152]{1,0:T(8,128)(2,1)S(1)}, bf16[128,1152]{1,0:T(8,128)(2,1)}, u32[]{:S(2)}) copy-start(bf16[128,1152]{1,0:T(8,128)(2,1)} %get-tuple-element.30) | copy-start | bytes 884740
  115.2 14.0 %copy-start = (bf16[128,1152]{1,0:T(8,128)(2,1)S(1)}, bf16[128,1152]{1,0:T(8,128)(2,1)}, u32[]{:S(2)}) copy-start(bf16[128,1152]{1,0:T(8,128)(2,1)} %get-tuple-element.31) | copy-start | bytes 884740
